TPU v7x, 256 devices: a whole 4x4x8 slice. The times are simulated.
256 devices in a mesh: grp: 4 (over z_hi), ctx: 64 (over z_lo, x, y, core).
Axes of the slice: x: 4, y: 4, z: 8 (z_hi: 4, z_lo: 2; z = z_hi * 2 + z_lo), core: 2. Of those that a mesh axis runs over, the one named last changes fastest.
Arguments:
- queries: bfloat16 [4, 12288, 1024], P('grp', 'ctx'), may hold values from -160 to 160
- grad_out: bfloat16 [4, 12288, 1024], P('grp', 'ctx'), may hold values from -6 to 6
- rollout_cache: bfloat16 [4, 12288, 256], P('grp', 'ctx'), may hold values from -8 to 8
- prompt_cache: bfloat16 [4, 4096, 256], P('grp', 'ctx'), may hold values from -6 to 6
- rollout_hidden: bfloat16 [4, 12288, 5120], P('grp', 'ctx'), may hold values from -6 to 6
- prompt_hidden: bfloat16 [4, 4096, 5120], P('grp', 'ctx'), may hold values from -16 to 16
- lengths: int32 [4, 128], P('grp', 'ctx'), may hold values from 24 to 96, as said below
Outputs:
- query_grad: bfloat16 [4, 12288, 1024], P('grp', 'ctx')
- rollout_grad: bfloat16 [4, 12288, 256], P('grp', 'ctx')
- prompt_grad: bfloat16 [4, 4096, 256], P('grp', 'ctx')
- weight_grad: float32 [5120, 256], P('ctx')
Inputs may be any that keep to these rules, and one draw needn't show every extreme that they name: `lengths`: in every group some rollout has exactly 96 tokens.
All inputs are finite; a program needn't handle non-finite values.
Results may differ from a plain program's by a relative error of at most 0.017.
Values may be sent and summed in bfloat16 or wider, within the bound.
A program may use at most 64 MiB of HBM per device.

v0:
```python
import math

import jax
import jax.numpy as jnp
from jax import lax
from jax.sharding import PartitionSpec as P


def pick_blocks(shards, shard_rows, limit):
    factor = max(1, min(shards, limit // shard_rows))
    while shards % factor:
        factor = factor - 1
    return factor


def body(queries, grad_out, rollout_cache, prompt_cache, rollout_hidden, prompt_hidden, lengths):
    width = prompt_cache.shape[2]
    head_size = width // 2
    head_count = queries.shape[2] // head_size
    slot_count = lengths.shape[1]
    capacity = queries.shape[1]
    slot_len = capacity // slot_count
    shard_rows = prompt_cache.shape[1]
    contexts = lax.axis_size("ctx")
    scaling = 1.0 / math.sqrt(head_size)
    total_rows = slot_count * head_count * slot_len

    def to_slots(tensor):
        return (
            tensor[0]
            .reshape(slot_count, slot_len, head_count, head_size)
            .transpose(0, 2, 1, 3)
            .reshape(slot_count, head_count * slot_len, head_size)
        )

    query_slots = to_slots(queries)
    grad_slots = to_slots(grad_out)
    query_rows = query_slots.reshape(total_rows, head_size)
    grad_rows = grad_slots.reshape(total_rows, head_size)
    rollout = rollout_cache[0].reshape(slot_count, slot_len, width)
    roll_keys = rollout[:, :, :head_size]
    roll_values = rollout[:, :, head_size:]
    limits = lengths[0]
    query_pos = lax.broadcasted_iota(jnp.int32, (slot_count, head_count, slot_len, slot_len), 2)
    key_pos = lax.broadcasted_iota(jnp.int32, (slot_count, head_count, slot_len, slot_len), 3)
    allowed = ((key_pos <= query_pos) & (key_pos < limits[:, None, None, None])).reshape(
        slot_count, head_count * slot_len, slot_len
    )
    token_pos = lax.broadcasted_iota(jnp.int32, (slot_count, head_count, slot_len), 2)
    live = (token_pos < limits[:, None, None]).reshape(total_rows).astype(jnp.float32)
    roll_scores = (
        jnp.einsum("sqd,skd->sqk", query_slots, roll_keys, preferred_element_type=jnp.float32)
        * scaling
    )
    roll_scores = jnp.where(allowed, roll_scores, -1e30)
    roll_dp = jnp.einsum(
        "sqd,skd->sqk", grad_slots, roll_values, preferred_element_type=jnp.float32
    )
    start_max = jnp.max(roll_scores, axis=2)
    roll_exp = jnp.exp(roll_scores - start_max[:, :, None])
    start_sum = jnp.sum(roll_exp, axis=2).reshape(total_rows)
    start_acc = jnp.sum(roll_exp * roll_dp, axis=2).reshape(total_rows)
    gathered = lax.all_gather(prompt_cache[0], "ctx", axis=0, tiled=True)
    per_block = pick_blocks(contexts, shard_rows, 512)
    block_rows = per_block * shard_rows
    blocks_total = contexts // per_block

    def scores_of(keyval):
        scores = (
            jnp.einsum(
                "rd,kd->rk", query_rows, keyval[:, :head_size], preferred_element_type=jnp.float32
            )
            * scaling
        )
        products = jnp.einsum(
            "rd,kd->rk", grad_rows, keyval[:, head_size:], preferred_element_type=jnp.float32
        )
        return (scores, products)

    def stats_step(index, carry):
        running, totals, weighted = carry
        keyval = lax.dynamic_slice_in_dim(gathered, index * block_rows, block_rows, 0)
        scores, products = scores_of(keyval)
        newest = jnp.maximum(running, jnp.max(scores, axis=1))
        shrink = jnp.exp(running - newest)
        weights = jnp.exp(scores - newest[:, None])
        return (
            newest,
            totals * shrink + jnp.sum(weights, axis=1),
            weighted * shrink + jnp.sum(weights * products, axis=1),
        )

    running, totals, weighted = lax.fori_loop(
        0, blocks_total, stats_step, (start_max.reshape(total_rows), start_sum, start_acc)
    )
    deltas = weighted / totals
    inverse = live / totals

    def block_grads(keyval):
        scores, products = scores_of(keyval)
        probs = jnp.exp(scores - running[:, None]) * inverse[:, None]
        dscore = (probs * (products - deltas[:, None])).astype(jnp.bfloat16)
        return (dscore, probs.astype(jnp.bfloat16))

    def cache_terms(keyval):
        dscore, probs = block_grads(keyval)
        key_part = (
            jnp.einsum("rk,rd->kd", dscore, query_rows, preferred_element_type=jnp.float32)
            * scaling
        )
        value_part = jnp.einsum("rk,rd->kd", probs, grad_rows, preferred_element_type=jnp.float32)
        return (dscore, jnp.concatenate([key_part, value_part], axis=1))

    slot_running = running.reshape(slot_count, head_count * slot_len)
    slot_inverse = inverse.reshape(slot_count, head_count * slot_len)
    slot_deltas = deltas.reshape(slot_count, head_count * slot_len)
    roll_probs = jnp.exp(roll_scores - slot_running[:, :, None]) * slot_inverse[:, :, None]
    roll_ds = (roll_probs * (roll_dp - slot_deltas[:, :, None])).astype(jnp.bfloat16)
    roll_pb = roll_probs.astype(jnp.bfloat16)
    roll_dq = jnp.einsum(
        "sqk,skd->sqd", roll_ds, roll_keys, preferred_element_type=jnp.float32
    ).reshape(total_rows, head_size)
    roll_dk = (
        jnp.einsum("sqk,sqd->skd", roll_ds, query_slots, preferred_element_type=jnp.float32)
        * scaling
    )
    roll_dv = jnp.einsum("sqk,sqd->skd", roll_pb, grad_slots, preferred_element_type=jnp.float32)
    rollout_flat = (
        jnp.concatenate([roll_dk, roll_dv], axis=2).reshape(capacity, width).astype(jnp.bfloat16)
    )

    def grad_step(index, carry):
        dquery, buffer = carry
        keyval = lax.dynamic_slice_in_dim(gathered, index * block_rows, block_rows, 0)
        dscore, terms = cache_terms(keyval)
        dquery = dquery + jnp.dot(dscore, keyval[:, :head_size], preferred_element_type=jnp.float32)
        return (dquery, lax.dynamic_update_slice_in_dim(buffer, terms, index * block_rows, 0))

    dquery, buffer = lax.fori_loop(
        0,
        blocks_total,
        grad_step,
        (jnp.zeros((total_rows, head_size), jnp.float32), jnp.zeros(gathered.shape, jnp.float32)),
    )
    prompt_sum = lax.psum_scatter(buffer, "ctx", scatter_dimension=0, tiled=True)
    dquery_total = (dquery + roll_dq) * scaling
    query_grad = (
        dquery_total.reshape(slot_count, head_count, slot_len, head_size)
        .transpose(0, 2, 1, 3)
        .reshape(1, capacity, head_count * head_size)
        .astype(jnp.bfloat16)
    )
    prompt_flat = prompt_sum.astype(jnp.bfloat16)
    prompt_states = prompt_hidden[0]
    rollout_states = rollout_hidden[0]
    local_sum = jnp.einsum(
        "tc,tw->cw", prompt_states, prompt_flat, preferred_element_type=jnp.float32
    )
    local_sum = local_sum + jnp.einsum(
        "tc,tw->cw", rollout_states, rollout_flat, preferred_element_type=jnp.float32
    )
    group_total = lax.psum(local_sum.astype(jnp.bfloat16), "grp").astype(jnp.float32)
    weight_grad = lax.psum_scatter(group_total, "ctx", scatter_dimension=0, tiled=True)
    return (query_grad, rollout_flat[None], prompt_flat[None], weight_grad)


def solution(mesh):
    in_specs = (
        P("grp", "ctx", None),
        P("grp", "ctx", None),
        P("grp", "ctx", None),
        P("grp", "ctx", None),
        P("grp", "ctx", None),
        P("grp", "ctx", None),
        P("grp", "ctx"),
    )
    out_specs = (
        P("grp", "ctx", None),
        P("grp", "ctx", None),
        P("grp", "ctx", None),
        P("ctx", None),
    )
    return jax.shard_map(body, mesh=mesh, in_specs=in_specs, out_specs=out_specs, check_vma=False)
```

profile of v0, /device:TPU:8, one launch (start us, length us, event | category | flops | bytes accessed | tf_op | source)
XLA Modules:
  0.0 938.7 jit_solution(9586681905796977793)
XLA Ops:
  12.6 105.3 %all-gather.3.cloned.1.call-done = bf16[1,4096,256]{2,1,0:T(8,128)(2,1)} async-done(((bf16[1,64,256]{2,1,0:T(8,128)(2,1)}), bf16[1,4096,256]{2,1,0:T(8,128)(2,1)}) %all-gather.3.cloned.1.call-update) | async-done | bytes 2097168 | tf_op jit(solution)/shard_map/all_gather | solution.py:63
  117.9 29.0 %while.33 = (s32[]{:T(128)}, f32[1536]{0:T(1024)S(1)}, f32[1536]{0:T(1024)S(1)}, f32[1536]{0:T(1024)S(1)}, bf16[4096,256]{1,0:T(8,128)(2,1)}, /*index=5*/bf16[15...) while((s32[]{:T(128)}, f32[1536]{0:T(1024)S(1)}, ...), condition=%wide.region_7.8_spmd, body=%wide.region_3.7_spmd.sunk | while | flops 408162816 | bytes 10596539 | solution.py:93
  119.4 1.6 fusion.83
  123.1 1.6 fusion.83
  126.7 1.6 fusion.83
  130.3 1.6 fusion.83
  134.0 1.6 fusion.83
  137.6 1.6 fusion.83
  141.2 1.6 fusion.83
  144.9 1.6 fusion.83
  147.0 2.2 broadcast_in_dim.28.clone
  149.2 81.0 %while.34 = (s32[]{:T(128)}, f32[1536,128]{1,0:T(8,128)}, f32[4096,256]{1,0:T(8,128)}, bf16[4096,256]{1,0:T(8,128)(2,1)}, bf16[1536,128]{1,0:T(8,128)(2,1)S(1)},...) while((s32[]{:T(128)}, f32[1536,128]{1,0:T(8,128)}, ...), condition=%wide.region_9.10_spmd.clone, body=%wide.region_8.9_spmd.clone.sunk | while | flops 1012727808 | bytes 21383396 | solution.py:139
  149.2 1.6 fusion.95
  151.5 1.5 fusion.96
  153.7 2.4 convolution_add_fusion.3
  157.2 1.9 constant_dynamic-update-slice_fusion.2
  159.1 1.6 fusion.95
  163.5 2.7 convolution_add_fusion.3
  167.3 1.9 constant_dynamic-update-slice_fusion.2
  169.2 1.6 fusion.95
  171.5 1.5 fusion.96
  173.7 2.7 convolution_add_fusion.3
  177.5 1.9 constant_dynamic-update-slice_fusion.2
  179.4 1.6 fusion.95
  181.7 1.5 fusion.96
  183.9 2.7 convolution_add_fusion.3
  187.7 1.9 constant_dynamic-update-slice_fusion.2
  189.6 1.6 fusion.95
  191.9 1.5 fusion.96
  194.1 2.7 convolution_add_fusion.3
  197.9 1.9 constant_dynamic-update-slice_fusion.2
  199.8 1.6 fusion.95
  202.1 1.5 fusion.96
  204.2 2.7 convolution_add_fusion.3
  208.0 1.9 constant_dynamic-update-slice_fusion.2
  209.9 1.6 fusion.95
  212.2 1.5 fusion.96
  214.4 2.7 convolution_add_fusion.3
  218.2 1.9 constant_dynamic-update-slice_fusion.2
  220.1 1.6 fusion.95
  224.6 2.7 convolution_add_fusion.3
  228.4 1.9 constant_dynamic-update-slice_fusion.2
  233.5 283.3 %reduce-scatter.5.cloned.1.call-done = f32[64,256]{1,0:T(8,128)} async-done(((f32[4096,256]{1,0:T(8,128)}), f32[64,256]{1,0:T(8,128)}) %reduce-scatter.5.cloned.1.call-update) | async-done | bytes 65552 | tf_op jit(solution)/shard_map/reduce_scatter | solution.py:145
  516.8 2.0 fusion.24
  518.8 2.5 fusion.18
  521.3 112.5 %all-reduce.2.cloned.1.call-done = bf16[5120,256]{0,1:T(8,128)(2,1)} async-done(((bf16[5120,256]{0,1:T(8,128)(2,1)}), bf16[5120,256]{0,1:T(8,128)(2,1)}) %all-reduce.2.cloned.1.call-update) | async-done | bytes 2621456 | tf_op jit(solution)/shard_map/psum | solution.py:162
  633.8 4.9 copy.21
  643.6 288.6 %reduce-scatter.7.cloned.1.call-done = f32[80,256]{1,0:T(8,128)} async-done(((f32[5120,256]{1,0:T(8,128)}), f32[80,256]{1,0:T(8,128)}) %reduce-scatter.7.cloned.1.call-update) | async-done | bytes 81936
  (125 shorter events, 51.5 us)
Async XLA Ops:
  7.2 511.6 %copy-start = (bf16[1,192,5120]{2,1,0:T(8,128)(2,1)S(1)}, bf16[1,192,5120]{2,1,0:T(8,128)(2,1)}, u32[]{:S(2)}) copy-start(bf16[1,192,5120]{2,1,0:T(8,128)(2,1)} %param.15) | copy-start | bytes 5898244
  7.2 4.0 copy-start.7
  7.2 4.0 copy-start.6
  7.2 110.7 %all-gather.3.cloned.1.call-start = ((), (), s32[]{:S(2)}) async-start(), calls=%async_computation.4 | async-start | bytes 2129920 | tf_op jit(solution)/shard_map/all_gather | solution.py:63
  7.9 508.8 %reduce-scatter.5.cloned.1.call-start = ((), (), s32[]{:S(2)}) async-start(), calls=%async_computation.2 | async-start | bytes 4259840 | tf_op jit(solution)/shard_map/reduce_scatter | solution.py:145
  11.5 106.5 %copy-start.1 = (f32[2,768,96]{1,2,0:T(8,128)}, f32[2,768,96]{1,2,0:T(8,128)S(1)}, u32[]{:S(2)}) copy-start(f32[2,768,96]{1,2,0:T(8,128)S(1)} %get-tuple-element.369) | copy-start | bytes 1769476
  230.2 1.1 copy-start.2
  230.3 403.5 %all-reduce.2.cloned.1.call-start = ((), (), s32[]{:S(2)}) async-start(), calls=%async_computation.3 | async-start | bytes 5242880 | tf_op jit(solution)/shard_map/psum | solution.py:162
  232.5 0.7 copy-start.3
  521.2 410.9 %reduce-scatter.7.cloned.1.call-start = ((), (), s32[]{:S(2)}) async-start(), calls=%async_computation.5 | async-start | bytes 5324800
  638.7 1.0 copy-start.4
  639.7 3.3 copy-start.5
Sparse Core Ops, SparseCore 0:
  9.9 107.9 all-gather.2
  230.4 286.3 reduce-scatter.4
  521.4 112.3 all-reduce.1
  638.8 293.2 reduce-scatter.6
where the time goes:
time: 946 us; the launch traced here: 939 us
  waiting for transfers between devices  790 us (84%)
  matrix products  88.3 us (9%)
  local copies, waits for them, and re-layouts  36.5 us (4%)
  between operations  14 us (1%)
    unnamed x5, waiting for transfers between devices  289 us
    reduce_scatter x1, waiting for transfers between devices, body(): lax.psum_scatter(buffer, 'ctx', scatter_dimension=0, tiled=True)  283 us
    psum x1, waiting for transfers between devices, body(): lax.psum(local_sum.astype(jnp.bfloat16), 'grp').astype(jnp.float32)  112 us
    all_gather x1, waiting for transfers between devices, body(): gathered = lax.all_gather(prompt_cache[0], 'ctx', axis=0, tiled=True)  105 us
    dot_general x16, matrix products, scores_of(): jnp.einsum('rd,kd->rk', query_rows, keyval[:, :head_size], preferred_elem...  24.8 us
    dot_general x16, matrix products, scores_of(): jnp.einsum('rd,kd->rk', grad_rows, keyval[:, head_size:], preferred_eleme...  24.7 us
    dynamic_update_slice x16, local copies, waits for them, and re-layouts, grad_step(): lax.dynamic_update_slice_in_dim(buffer, terms, index * block_rows, 0)  23.4 us
    dot_general x8, matrix products, grad_step(): jnp.dot(dscore, keyval[:, :head_size], preferred_element_type=jnp.float32)  21.5 us
  transfers between devices with their start and end apart: 4, of which 4 were waited for; matrix products, arithmetic and copies ran while one was open for 1% of the time, Pallas kernels for 0%

commit v1 on v0

v1 whole, which is shorter than its diff:
```python
import math

import jax
import jax.numpy as jnp
from jax import lax
from jax.experimental import pallas as pl
from jax.experimental.pallas import tpu as pltpu
from jax.sharding import PartitionSpec as P

MESH = pl.DeviceIdType.MESH
F32, BF16 = jnp.float32, jnp.bfloat16
KEYS, ROLL, ROWS, HD = 4096, 192, 1536, 128
CHUNK, TILE = 512, 256
SCALE = 1.0 / math.sqrt(HD)


def dot(a, b):
    return jnp.dot(a, b, preferred_element_type=F32)


def dot_nt(a, b):
    return lax.dot_general(a, b, (((1,), (1,)), ((), ())), preferred_element_type=F32)


def dot_tn(a, b):
    return lax.dot_general(a, b, (((0,), (0,)), ((), ())), preferred_element_type=F32)


class Place:
    def __init__(self):
        self.g = lax.axis_index("grp")
        t = lax.axis_index("ctx")
        self.t = t
        self.c = lax.rem(t, 2)
        y = lax.rem(t // 2, 4)
        x = lax.rem(t // 8, 4)
        z = t // 32
        a = x + self.c * (y - x)
        self.b = y + self.c * (x - y)
        self.other_b = x + self.c * (y - x)
        self.s = a * 2 + z

    def dev(self, b, s):
        a, z = s // 2, lax.rem(s, 2)
        x = a + self.c * (b - a)
        y = b + self.c * (a - b)
        return (self.g, z * 32 + x * 8 + y * 2 + self.c)

    def core(self):
        return (self.g, self.t + 1 - 2 * self.c)

    def near(self, j):
        return self.dev(self.b, lax.rem(self.s + j, 8))

    def up(self):
        return self.dev(lax.rem(self.b + 1, 4), self.s)

    def down(self):
        return self.dev(lax.rem(self.b + 3, 4), self.s)

    def group(self, j):
        return (lax.rem(self.g + j, 4), self.t)

    def partners(self):
        return [self.core(), self.up(), self.down()] + [self.near(j) for j in range(1, 8)]


def barrier(devices):
    sem = pltpu.get_barrier_semaphore()
    for device in devices:
        pl.semaphore_signal(sem, inc=1, device_id=device, device_id_type=MESH)
    pl.semaphore_wait(sem, len(devices))


def remote(src, dst, send, recv, device):
    return pltpu.make_async_remote_copy(
        src_ref=src, dst_ref=dst, send_sem=send, recv_sem=recv, device_id=device, device_id_type=MESH
    )


def gather_kernel(cache_ref, kv, send, recv, recv_core):
    here = Place()
    base = here.c * 32
    copies = []

    def push(pos, sems, device, into):
        copy = remote(kv.at[pos], kv.at[pos], send.at[len(copies)], into, device)
        copy.start()
        copies.append(copy)

    def arrived(pos, sem):
        remote(kv.at[pos], kv.at[pos], send.at[0], sem, here.core()).wait_recv()

    def block(b, s):
        return lax.rem(here.b + b, 4) * 8 + s

    own = block(0, here.s)
    kv[base + own] = cache_ref[...]
    barrier(here.partners())
    for j in range(1, 8):
        push(base + own, None, here.near(j), recv.at[own])
    order = [lax.rem(here.s + 8 - i, 8) for i in range(8)]
    for i in range(8):
        at = block(0, order[i])
        if i:
            arrived(base + at, recv.at[at])
        push(base + at, None, here.up(), recv.at[at])
        push(base + at, None, here.down(), recv.at[at])
        push(base + at, None, here.core(), recv_core.at[at])
    for i in range(8):
        low, high = block(3, order[i]), block(1, order[i])
        arrived(base + low, recv.at[low])
        if i < 4:
            push(base + low, None, here.up(), recv.at[low])
        push(base + low, None, here.core(), recv_core.at[low])
        arrived(base + high, recv.at[high])
        if i >= 4:
            push(base + high, None, here.down(), recv.at[high])
        push(base + high, None, here.core(), recv_core.at[high])
    for i in range(8):
        at = block(2, order[i])
        arrived(base + at, recv.at[at])
        push(base + at, None, here.core(), recv_core.at[at])
    for at in range(32):
        arrived(32 - base + at, recv_core.at[at])
    for copy in copies:
        copy.wait_send()


def gather(cache):
    return pl.pallas_call(
        gather_kernel,
        out_shape=jax.ShapeDtypeStruct((64, 64, 256), BF16),
        in_specs=[pl.BlockSpec(memory_space=pltpu.VMEM)],
        out_specs=pl.BlockSpec(memory_space=pltpu.VMEM),
        scratch_shapes=[
            pltpu.SemaphoreType.DMA((63,)),
            pltpu.SemaphoreType.DMA((32,)),
            pltpu.SemaphoreType.DMA((32,)),
        ],
        compiler_params=pltpu.CompilerParams(collective_id=0, has_side_effects=True),
    )(cache)


def attention_kernel(len_ref, q_ref, g_ref, rc_ref, kv_ref, dq_ref, dr_ref, dp_ref, qa, ga, kt, S, DP, PB, DS):
    C = math.log2(math.e) * SCALE
    for h in range(8):
        qa[h * ROLL : (h + 1) * ROLL, :] = q_ref[:, h * HD : (h + 1) * HD]
        ga[h * ROLL : (h + 1) * ROLL, :] = g_ref[:, h * HD : (h + 1) * HD]
    for c in range(KEYS // CHUNK):
        kt[:, c * CHUNK : (c + 1) * CHUNK] = kv_ref[c * CHUNK : (c + 1) * CHUNK, :HD].T
    roll_kt = rc_ref[:, :HD].T
    n0, n1 = len_ref[0, 0], len_ref[0, 1]
    parts = [(c * CHUNK, CHUNK) for c in range(KEYS // CHUNK)] + [(KEYS, ROLL)]

    def fold(v, op):
        return op(v.reshape(v.shape[0] // 8, 8, TILE), axis=0)

    def tile(rt, _):
        r0 = pl.multiple_of(rt * TILE, TILE)
        q, g = qa[pl.ds(r0, TILE), :], ga[pl.ds(r0, TILE), :]
        rows = lax.broadcasted_iota(jnp.int32, (1, TILE), 1) + r0
        w = lax.rem(rows, ROLL)
        row_slot = (w >= 96).astype(jnp.int32)
        t = w - 96 * row_slot
        lim = jnp.where(row_slot == 1, n1, n0)
        live = (t < lim).astype(F32)
        keys = lax.broadcasted_iota(jnp.int32, (ROLL, 1), 0)
        key_slot = (keys >= 96).astype(jnp.int32)
        u = keys - 96 * key_slot
        ok = (key_slot == row_slot) & (u <= t) & (u < lim)
        s = jnp.where(ok, dot_nt(rc_ref[:, :HD], q), -1e30)
        S[KEYS:, :] = s
        top = fold(s, jnp.max)
        for at, size in parts[:-1]:
            s = dot_nt(kv_ref[at : at + size, :HD], q)
            S[at : at + size, :] = s
            top = jnp.maximum(top, fold(s, jnp.max))
        top = jnp.max(top, axis=0, keepdims=True) * C
        total = jnp.zeros((8, TILE), F32)
        weighted = jnp.zeros((8, TILE), F32)
        for at, size in parts:
            v = kv_ref[at : at + size, HD:] if at < KEYS else rc_ref[:, HD:]
            d = dot_nt(v, g)
            e = jnp.exp2(S[at : at + size, :] * C - top)
            S[at : at + size, :] = e
            DP[at : at + size, :] = d
            total = total + fold(e, jnp.sum)
            weighted = weighted + fold(e * d, jnp.sum)
        total = jnp.sum(total, axis=0, keepdims=True)
        delta = jnp.sum(weighted, axis=0, keepdims=True) / total
        inv = live / total
        acc = jnp.zeros((HD, TILE), F32)
        for at, size in parts:
            p = S[at : at + size, :] * inv
            ds = (p * (DP[at : at + size, :] - delta)).astype(BF16)
            PB[at : at + size, pl.ds(r0, TILE)] = p.astype(BF16)
            DS[at : at + size, pl.ds(r0, TILE)] = ds
            acc = acc + dot(kt[:, at : at + size] if at < KEYS else roll_kt, ds)
        dq_ref[pl.ds(r0, TILE), :] = (acc.T * SCALE).astype(BF16)
        return 0

    lax.fori_loop(0, ROWS // TILE, tile, 0)

    def grads(at):
        return jnp.concatenate([dot(DS[at, :], qa[...]) * SCALE, dot(PB[at, :], ga[...])], axis=1).astype(BF16)

    dr_ref[...] = grads(slice(KEYS, KEYS + ROLL))

    def key_tile(c, _):
        at = pl.ds(pl.multiple_of(c * TILE, TILE), TILE)
        dp_ref[at, :] = grads(at)
        return 0

    lax.fori_loop(0, KEYS // TILE, key_tile, 0)


def attention(lengths, q, g, cache, kv):
    vmem = pl.BlockSpec(memory_space=pltpu.VMEM)
    return pl.pallas_call(
        attention_kernel,
        out_shape=(
            jax.ShapeDtypeStruct((ROWS, HD), BF16),
            jax.ShapeDtypeStruct((ROLL, 2 * HD), BF16),
            jax.ShapeDtypeStruct((KEYS, 2 * HD), BF16),
        ),
        in_specs=[pl.BlockSpec(memory_space=pltpu.SMEM)] + [vmem] * 4,
        out_specs=(vmem,) * 3,
        scratch_shapes=[
            pltpu.VMEM((ROWS, HD), BF16),
            pltpu.VMEM((ROWS, HD), BF16),
            pltpu.VMEM((HD, KEYS), BF16),
            pltpu.VMEM((KEYS + ROLL, TILE), F32),
            pltpu.VMEM((KEYS + ROLL, TILE), F32),
            pltpu.VMEM((KEYS + ROLL, ROWS), BF16),
            pltpu.VMEM((KEYS + ROLL, ROWS), BF16),
        ],
        compiler_params=pltpu.CompilerParams(vmem_limit_bytes=60 << 20),
    )(lengths, q, g, cache, kv)


class Scatter:
    def __init__(self, here, buf, r0, ra, rb, r2a, r2b, r3, send, recv):
        self.here, self.buf, self.r0, self.ra, self.rb = here, buf, r0, ra, rb
        self.r2a, self.r2b, self.r3, self.send, self.recv = r2a, r2b, r3, send, recv
        self.copies = []

    def push(self, src, dst, sem, device):
        copy = remote(src, dst, self.send.at[len(self.copies)], self.recv.at[sem], device)
        copy.start()
        self.copies.append(copy)

    def got(self, dst, sem):
        remote(dst, dst, self.send.at[0], self.recv.at[sem], self.here.core()).wait_recv()

    def start(self):
        here = self.here
        for i, b in enumerate((2, 1, 3, 0)):
            at = lax.rem(here.other_b + b, 4) * 8
            self.push(self.buf.at[pl.ds(32 - here.c * 32 + at, 8)], self.r0.at[pl.ds(at, 8)], i, here.core())

    def finish(self):
        here = self.here
        base = here.c * 32

        def merge(i, b):
            at = lax.rem(here.b + b, 4) * 8
            self.got(self.r0.at[pl.ds(at, 8)], i)
            return at

        def add(at, k):
            total = self.buf[base + at + k].astype(F32) + self.r0[at + k].astype(F32)
            self.r0[at + k] = total.astype(BF16)

        far = merge(0, 2)
        for k in range(8):
            add(far, k)
        self.push(self.r0.at[pl.ds(far, 4)], self.ra, 4, here.up())
        self.push(self.r0.at[pl.ds(far + 4, 4)], self.rb, 5, here.down())
        up = merge(1, 1)
        for k in range(4, 8):
            add(up, k)
        self.push(self.r0.at[pl.ds(up + 4, 4)], self.r2a.at[pl.ds(4, 4)], 6, here.up())
        down = merge(2, 3)
        for k in range(4):
            add(down, k)
        self.push(self.r0.at[pl.ds(down, 4)], self.r2b.at[pl.ds(0, 4)], 7, here.down())
        self.got(self.ra, 4)
        for k in range(4):
            total = self.buf[base + up + k].astype(F32) + self.r0[up + k].astype(F32) + self.ra[k].astype(F32)
            self.r0[up + k] = total.astype(BF16)
        self.push(self.r0.at[pl.ds(up, 4)], self.r2a.at[pl.ds(0, 4)], 8, here.up())
        self.got(self.rb, 5)
        for k in range(4, 8):
            total = self.buf[base + down + k].astype(F32) + self.r0[down + k].astype(F32) + self.rb[k - 4].astype(F32)
            self.r0[down + k] = total.astype(BF16)
        self.push(self.r0.at[pl.ds(down + 4, 4)], self.r2b.at[pl.ds(4, 4)], 9, here.down())
        mine = merge(3, 0)
        self.got(self.r2a.at[pl.ds(4, 4)], 6)
        self.got(self.r2b.at[pl.ds(0, 4)], 7)
        self.got(self.r2a.at[pl.ds(0, 4)], 8)
        self.got(self.r2b.at[pl.ds(4, 4)], 9)

        def own(k):
            return (
                self.buf[base + mine + k].astype(F32)
                + self.r0[mine + k].astype(F32)
                + self.r2a[k].astype(F32)
                + self.r2b[k].astype(F32)
            )

        for j in range(1, 8):
            k = lax.rem(here.s + j, 8)
            self.r0[mine + k] = own(k).astype(BF16)
            self.push(self.r0.at[mine + k], self.r3.at[here.s], 10 + j, here.near(j))
        total = own(here.s)
        for j in range(1, 8):
            k = lax.rem(here.s + j, 8)
            self.got(self.r3.at[k], 10 + 8 - j)
            total = total + self.r3[k].astype(F32)
        return total

    def drain(self):
        for copy in self.copies:
            copy.wait_send()


def scatter_scratch(n):
    return [
        pltpu.VMEM((32, n, 256), BF16),
        pltpu.VMEM((4, n, 256), BF16),
        pltpu.VMEM((4, n, 256), BF16),
        pltpu.VMEM((8, n, 256), BF16),
        pltpu.VMEM((8, n, 256), BF16),
        pltpu.VMEM((8, n, 256), BF16),
        pltpu.SemaphoreType.DMA((17,)),
        pltpu.SemaphoreType.DMA((18,)),
    ]


def weight_kernel(dp_ref, dr_ref, hr_ref, hp_ref, pg_ref, w_ref, w1, wb, wg, gsend, grecv, *scratch):
    here = Place()
    prompt = Scatter(here, dp_ref, *scratch[:8])
    weight = Scatter(here, wb, *scratch[8:])
    barrier(here.partners() + [here.group(j) for j in range(1, 4)])
    prompt.start()
    for k in range(8):
        cols = slice(k * 640, (k + 1) * 640)
        w1[cols, :] = dot_tn(hr_ref[:, cols], dr_ref[...])
    own = prompt.finish().astype(BF16)
    pg_ref[...] = own
    for k in range(8):
        cols = slice(k * 640, (k + 1) * 640)
        part = (w1[cols, :] + dot_tn(hp_ref[:, cols], own)).astype(BF16)
        z, x = k // 4, k % 4
        for y in range(4):
            for c in range(2):
                a, b = (x, y) if c == 0 else (y, x)
                i = y * 2 + c
                wb[c * 32 + b * 8 + a * 2 + z] = part[i * 80 : (i + 1) * 80]
    weight.start()
    total = weight.finish()
    wg[0] = total.astype(BF16)
    copies = []
    for j in range(1, 4):
        copy = remote(wg.at[0], wg.at[4 - j], gsend.at[j], grecv.at[4 - j], here.group(j))
        copy.start()
        copies.append(copy)
    for j in range(1, 4):
        remote(wg.at[0], wg.at[j], gsend.at[j], grecv.at[j], here.group(j)).wait_recv()
        total = total + wg[j].astype(F32)
    w_ref[...] = total
    for copy in copies:
        copy.wait_send()
    prompt.drain()
    weight.drain()


def weights(dp, dr, hr, hp):
    vmem = pl.BlockSpec(memory_space=pltpu.VMEM)
    return pl.pallas_call(
        weight_kernel,
        out_shape=(jax.ShapeDtypeStruct((64, 256), BF16), jax.ShapeDtypeStruct((80, 256), F32)),
        in_specs=[vmem] * 4,
        out_specs=(vmem,) * 2,
        scratch_shapes=[
            pltpu.VMEM((5120, 256), F32),
            pltpu.VMEM((64, 80, 256), BF16),
            pltpu.VMEM((4, 80, 256), BF16),
            pltpu.SemaphoreType.DMA((4,)),
            pltpu.SemaphoreType.DMA((4,)),
        ]
        + scatter_scratch(64)
        + scatter_scratch(80),
        compiler_params=pltpu.CompilerParams(
            collective_id=1, has_side_effects=True, vmem_limit_bytes=56 << 20
        ),
    )(dp, dr, hr, hp)


def body(queries, grad_out, rollout_cache, prompt_cache, rollout_hidden, prompt_hidden, lengths):
    kv = gather(prompt_cache[0]).reshape(KEYS, 2 * HD)
    dq, dr, dp = attention(lengths, queries[0], grad_out[0], rollout_cache[0], kv)
    pg, w = weights(dp.reshape(64, 64, 256), dr, rollout_hidden[0], prompt_hidden[0])
    query_grad = dq.reshape(8, ROLL, HD).transpose(1, 0, 2).reshape(1, ROLL, 8 * HD)
    return (query_grad, dr[None], pg[None], w)


def solution(mesh):
    rows = P("grp", "ctx", None)
    in_specs = (rows,) * 6 + (P("grp", "ctx"),)
    out_specs = (rows, rows, rows, P("ctx", None))
    return jax.shard_map(body, mesh=mesh, in_specs=in_specs, out_specs=out_specs, check_vma=False)
```

time: 946 us -> 114 us (0.12)
  waiting for transfers between devices: 790 us -> 0 us
  Pallas kernels: 0 us -> 108 us
  matrix products: 88.3 us -> 0 us
  local copies, waits for them, and re-layouts: 36.5 us -> 5.07 us
  between operations: 14 us -> 0.65 us
    unnamed x5 -> x0, waiting for transfers between devices: 289 us -> none
    reduce_scatter x1 -> x0, waiting for transfers between devices: 283 us -> none  [body(): lax.psum_scatter(buffer, 'ctx', scatter_dimension=0, tiled=True)]
    psum x1 -> x0, waiting for transfers between devices: 112 us -> none  [body(): lax.psum(local_sum.astype(jnp.bfloat16), 'grp').astype(jnp.float32)]
    pallas_call x0 -> x3, Pallas kernels: none -> 108 us  [the longest x1 48.7 us: weights(): pl.pallas_call(weight_kernel, out_shape=(jax.ShapeDtypeStruct((64, 256),...]
    all_gather x1 -> x0, waiting for transfers between devices: 105 us -> none  [body(): gathered = lax.all_gather(prompt_cache[0], 'ctx', axis=0, tiled=True)]
    dot_general x63 -> x0, matrix products: 88.3 us -> none  [the longest x16 24.8 us: scores_of(): jnp.einsum('rd,kd->rk', query_rows, keyval[:, :head_size], preferred_elem...]
    dynamic_update_slice x16 -> x0, local copies, waits for them, and re-layouts: 23.4 us -> none  [grad_step(): lax.dynamic_update_slice_in_dim(buffer, terms, index * block_rows, 0)]
  transfers between devices with their start and end apart: 4 -> 0, of which waited for: 4 -> 0; matrix products, arithmetic and copies ran while one was open for 1% -> 0% of each run, Pallas kernels for 0% -> 0%
where the time goes in v1:
time: 114 us; the launch traced here: 113 us
  Pallas kernels  108 us (95%)
  local copies, waits for them, and re-layouts  5.07 us (4%)
    pallas_call x1, Pallas kernels, weights(): pl.pallas_call(weight_kernel, out_shape=(jax.ShapeDtypeStruct((64, 256),...  48.7 us
    pallas_call x1, Pallas kernels, attention(): pl.pallas_call(attention_kernel, out_shape=(jax.ShapeDtypeStruct((ROWS, H...  37.9 us
    pallas_call x1, Pallas kernels, gather(): pl.pallas_call(gather_kernel, out_shape=jax.ShapeDtypeStruct((64, 64, 256...  21 us
    unnamed x2, local copies, waits for them, and re-layouts  2.9 us

profile of v1, /device:TPU:8, one launch (start us, length us, event | category | flops | bytes accessed | tf_op | source)
XLA Modules:
  0.0 113.3 jit_solution(5848901928435678418)
XLA Ops:
  0.6 21.0 %shard_map.102 = bf16[64,64,256]{2,1,0:T(8,128)(2,1)} custom-call(bf16[64,256]{1,0:T(8,128)(2,1)} %bitcast.22), custom_call_target="tpu_custom_call" | custom-call | tf_op jit(solution)/shard_map/pallas_call | solution.py:131
  21.6 37.9 %shard_map.103 = (bf16[1536,128]{1,0:T(8,128)(2,1)}, bf16[192,256]{1,0:T(8,128)(2,1)}, bf16[4096,256]{1,0:T(8,128)(2,1)}) custom-call(s32[1,2]{1,0:T(1,128)} %len_ref.1, bf16[192,1024]{1,0:T(8,128)(2,1)} %bitcast.17, bf16[192,1024]{1,0:T(8,128)(2,1)} %bitcast.18, bf16[192,256]{1,0:T(8,128)(2,1)} %bitcast.20, bf16[4096,256]{1,0:T(8,128)(2,1)} %bitcast.13), custom_call_target="tpu_custom_call" | custom-call | tf_op jit(solution)/shard_map/pallas_call | solution.py:220
  59.5 1.3 %copy.11 = bf16[192,8,128]{2,1,0:T(8,128)(2,1)S(1)} copy(bf16[192,8,128]{2,0,1:T(8,128)(2,1)} %bitcast.19) | data formatting | bytes 786432 | tf_op jit(solution)/shard_map/transpose | solution.py:405
  60.7 0.9 reshape.22
  61.6 48.7 %shard_map.104 = (bf16[64,256]{1,0:T(8,128)(2,1)}, f32[80,256]{1,0:T(8,128)}) custom-call(bf16[64,64,256]{2,1,0:T(8,128)(2,1)} %bitcast.14, bf16[192,256]{1,0:T(8,128)(2,1)} %get-tuple-element.10.dr_ref, bf16[192,5120]{1,0:T(8,128)(2,1)} %bitcast.15, bf16[64,5120]{1,0:T(8,128)(2,1)} %bitcast.16), custom_call_target="tpu_custom_call" | custom-call | tf_op jit(solution)/shard_map/pallas_call | solution.py:381
  110.4 1.4 %copy.14 = bf16[1,64,256]{2,1,0:T(8,128)(2,1)} copy(bf16[1,64,256]{2,1,0:T(8,128)(2,1)} %bitcast.23) | data formatting | bytes 65536
  111.7 1.5 %copy.15 = f32[80,256]{1,0:T(8,128)} copy(f32[80,256]{1,0:T(8,128)} %get-tuple-element.21) | data formatting | bytes 163840

commit v2 on v0

v2 whole, which is shorter than its diff:
```python
import math

import jax
import jax.numpy as jnp
from jax import lax
from jax.experimental import pallas as pl
from jax.experimental.pallas import tpu as pltpu
from jax.sharding import PartitionSpec as P

MESH = pl.DeviceIdType.MESH
F32, BF16 = jnp.float32, jnp.bfloat16
KEYS, ROLL, ROWS, HD, HEADS = 4096, 192, 1536, 128, 8
CHUNK, TILE = 256, 256
SCALE = 1.0 / math.sqrt(HD)
EXP_SCALE = math.log2(math.e) * SCALE


def dot(a, b):
    return jnp.dot(a, b, preferred_element_type=F32)


def dot_nt(a, b):
    return lax.dot_general(a, b, (((1,), (1,)), ((), ())), preferred_element_type=F32)


class Place:
    def __init__(self):
        self.g = lax.axis_index("grp")
        t = lax.axis_index("ctx")
        self.t = t
        self.c = lax.rem(t, 2)
        y = lax.rem(t // 2, 4)
        x = lax.rem(t // 8, 4)
        self.z = t // 32
        self.a = x + self.c * (y - x)
        self.b = y + self.c * (x - y)
        self.s = self.a * 2 + self.z

    def dev(self, a, b, z, core):
        x = a + self.c * (b - a)
        y = b + self.c * (a - b)
        return (self.g, z * 32 + x * 8 + y * 2 + core)

    def ring(self, i):
        return self.dev(self.a, lax.rem(self.b + i, 4), self.z, self.c)

    def near(self, j):
        s = lax.rem(self.s + j, 8)
        return self.dev(s // 2, self.b, lax.rem(s, 2), self.c)

    def cross_a(self, i):
        return self.dev(lax.rem(self.a + i, 4), self.b, self.z, 1 - self.c)

    def cross_b(self, i):
        return self.dev(self.a, lax.rem(self.b + i, 4), self.z, 1 - self.c)

    def group(self, j):
        return (lax.rem(self.g + j, 4), self.t)

    def partners(self):
        ring = [self.ring(i) for i in range(1, 4)]
        near = [self.near(j) for j in range(1, 8)]
        cross = [self.cross_a(i) for i in range(4)] + [self.cross_b(i) for i in range(1, 4)]
        return ring + near + cross + [self.group(j) for j in range(1, 4)]


def barrier(devices):
    sem = pltpu.get_barrier_semaphore()
    for device in devices:
        pl.semaphore_signal(sem, inc=1, device_id=device, device_id_type=MESH)
    pl.semaphore_wait(sem, len(devices))


class Net:
    def __init__(self, send, here):
        self.send, self.here, self.copies = send, here, []

    def copy(self, src, dst, sem, recv, device):
        return pltpu.make_async_remote_copy(
            src_ref=src, dst_ref=dst, send_sem=sem, recv_sem=recv, device_id=device, device_id_type=MESH
        )

    def push(self, src, dst, recv, device):
        copy = self.copy(src, dst, self.send.at[len(self.copies)], recv, device)
        copy.start()
        self.copies.append(copy)

    def got(self, dst, recv):
        self.copy(dst, dst, self.send.at[0], recv, self.here.cross_a(0)).wait_recv()

    def drain(self):
        for copy in self.copies:
            copy.wait_send()


SENDS = 63 + 7 + 7 + 7 + 17 + 7 + 3


def kernel(
    len_ref, q_ref, g_ref, rc_ref, cache_ref, hr_ref, hp_ref,
    dq_ref, dr_ref, pg_ref, w_ref,
    qa, ga, rc, hbuf, kv, kt, E, DP, PB, DS, dq, dp, ht, hx, grad, acc, wpart,
    r0, ra, rb, r2a, r2b, r3, wr3, wg,
    local, send, near_sem, core_sem, h_sem, gr_sem, gp_sem, s0_sem, s1_sem, s2_sem, w_sem, wg_sem,
):
    here = Place()
    net = Net(send, here)
    loads = []

    def load(src, dst):
        copy = pltpu.make_async_copy(src, dst, local.at[len(loads)])
        copy.start()
        loads.append(copy)

    load(cache_ref, kv.at[0])
    load(hr_ref, hbuf.at[pl.ds(0, ROLL)])
    load(hp_ref, hbuf.at[pl.ds(ROLL, 64)])
    load(rc_ref, rc)
    for h in range(HEADS):
        rows, cols = pl.ds(h * ROLL, ROLL), pl.ds(h * HD, HD)
        load(q_ref.at[:, cols], qa.at[rows])
        load(g_ref.at[:, cols], ga.at[rows])
    barrier(here.partners())

    loads[0].wait()
    core = here.cross_a(0)
    up, down = here.ring(1), here.ring(3)
    for j in range(1, 8):
        net.push(kv.at[0], kv.at[8 - j], near_sem.at[8 - j], here.near(j))

    def spread(j):
        net.push(kv.at[j], kv.at[24 + j], near_sem.at[24 + j], up)
        net.push(kv.at[j], kv.at[8 + j], near_sem.at[8 + j], down)
        net.push(kv.at[j], kv.at[32 + j], core_sem.at[j], core)

    def arrived(k):
        net.got(kv.at[k], near_sem.at[k])

    def to_core(k):
        net.push(kv.at[k], kv.at[32 + k], core_sem.at[k], core)

    spread(0)
    for j in range(1, 8):
        arrived(j)
        spread(j)

    loads[1].wait()
    loads[2].wait()
    for k in range(8):
        z, x = k // 4, k % 4
        part = hbuf[:, k * 640 : (k + 1) * 640].T.reshape(4, 2, 80, 256)
        for y in range(4):
            ht[0, y, z, x] = part[y, 0]
            ht[1, x, z, y] = part[y, 1]
        if k < 8:
            arrived(24 + k)
            if k < 4:
                net.push(kv.at[24 + k], kv.at[16 + k], near_sem.at[16 + k], up)
            to_core(24 + k)
            arrived(8 + k)
            if k >= 4:
                net.push(kv.at[8 + k], kv.at[16 + k], near_sem.at[16 + k], down)
            to_core(8 + k)
    for k in range(16, 24):
        arrived(k)
        to_core(k)
    for i in range(1, 4):
        net.push(ht.at[here.c, lax.rem(here.b + i, 4)], hx.at[4 - i], h_sem.at[4 - i], here.ring(i))
    for i in range(4):
        slot = 4 + (4 - i) % 4
        net.push(ht.at[1 - here.c, lax.rem(here.a + i, 4)], hx.at[slot], h_sem.at[slot], here.cross_a(i))
    for k in range(32):
        net.got(kv.at[32 + k], core_sem.at[k])
    for copy in loads[3:]:
        copy.wait()

    def keys(at, size):
        return kv[at // 64 : (at + size) // 64, :, :HD].reshape(size, HD)

    def values(at, size):
        return kv[at // 64 : (at + size) // 64, :, HD:].reshape(size, HD)

    for c in range(8):
        kt[:, c * 512 : (c + 1) * 512] = keys(c * 512, 512).T
    roll_kt = rc[:, :HD].T
    n0, n1 = len_ref[0, 0], len_ref[0, 1]
    parts = [(c * CHUNK, CHUNK) for c in range(KEYS // CHUNK)] + [(KEYS, ROLL)]
    for r0_ in range(0, ROWS, TILE):
        q, g = qa[r0_ : r0_ + TILE, :], ga[r0_ : r0_ + TILE, :]
        rows = lax.broadcasted_iota(jnp.int32, (1, TILE), 1) + r0_
        w = lax.rem(rows, ROLL)
        row_slot = (w >= 96).astype(jnp.int32)
        t = w - 96 * row_slot
        lim = jnp.where(row_slot == 1, n1, n0)
        live = (t < lim).astype(F32)
        idx = lax.broadcasted_iota(jnp.int32, (ROLL, 1), 0)
        key_slot = (idx >= 96).astype(jnp.int32)
        u = idx - 96 * key_slot
        ok = (key_slot == row_slot) & (u <= t) & (u < lim)
        top = jnp.full((8, TILE), -1e30, F32)
        total = jnp.zeros((8, TILE), F32)
        weighted = jnp.zeros((8, TILE), F32)
        tops = []
        for at, n in parts:
            if at < KEYS:
                s = dot_nt(keys(at, n), q) * EXP_SCALE
                d = dot_nt(values(at, n), g)
            else:
                s = jnp.where(ok, dot_nt(rc[:, :HD], q) * EXP_SCALE, -1e30)
                d = dot_nt(rc[:, HD:], g)
            s = s.reshape(n // 8, 8, TILE)
            newest = jnp.maximum(top, jnp.max(s, axis=0))
            shrink = jnp.exp2(top - newest)
            top = newest
            e = jnp.exp2(s - top[None])
            E[at : at + n, :] = e.reshape(n, TILE)
            DP[at : at + n, :] = d
            total = total * shrink + jnp.sum(e, axis=0)
            weighted = weighted * shrink + jnp.sum(e * d.reshape(n // 8, 8, TILE), axis=0)
            tops.append(top)
        highest = jnp.max(top, axis=0, keepdims=True)
        last = jnp.exp2(top - highest)
        sums = jnp.sum(total * last, axis=0, keepdims=True)
        delta = jnp.broadcast_to(jnp.sum(weighted * last, axis=0, keepdims=True) / sums, (8, TILE))
        inv = live / sums
        turned = jnp.zeros((HD, TILE), F32)
        for (at, n), old in zip(parts, tops):
            factor = jnp.exp2(old - highest) * inv
            p = E[at : at + n, :].reshape(n // 8, 8, TILE) * factor[None]
            ds = (p * (DP[at : at + n, :].reshape(n // 8, 8, TILE) - delta[None])).reshape(n, TILE).astype(BF16)
            PB[at : at + n, r0_ : r0_ + TILE] = p.reshape(n, TILE).astype(BF16)
            DS[at : at + n, r0_ : r0_ + TILE] = ds
            turned = turned + dot(kt[:, at : at + n] if at < KEYS else roll_kt, ds)
        dq[r0_ : r0_ + TILE, :] = (turned.T * SCALE).astype(BF16)
    stores = []
    for h in range(HEADS):
        rows, cols = pl.ds(h * ROLL, ROLL), pl.ds(h * HD, HD)
        copy = pltpu.make_async_copy(dq.at[rows], dq_ref.at[:, cols], local.at[len(loads) + h])
        copy.start()
        stores.append(copy)

    def grads(at, n):
        both = [dot(DS[at : at + n, :], qa[...]) * SCALE, dot(PB[at : at + n, :], ga[...])]
        return jnp.concatenate(both, axis=1).astype(BF16)

    def share(src, dst, sems):
        for i in range(1, 4):
            net.push(src(0), dst(4 - i), sems.at[4 - i], here.ring(i))
        for i in range(4):
            slot = 4 + (4 - i) % 4
            net.push(src(0), dst(slot), sems.at[slot], here.cross_a(i))

    def roll_part(k):
        return grad.at[k, pl.ds(0, ROLL)]

    def prompt_part(k):
        return grad.at[k, pl.ds(ROLL, 64)]

    mine = grads(KEYS, ROLL)
    dr_ref[...] = mine
    grad[0, :ROLL] = mine
    share(roll_part, roll_part, gr_sem)

    def block(k):
        dp[k * 8 : (k + 1) * 8] = grads(k * 512, 512).reshape(8, 64, 256)

    for i, b in enumerate((2, 1, 3, 0)):
        block(4 + b)
        net.push(dp.at[pl.ds(32 + b * 8, 8)], r0.at[pl.ds(b * 8, 8)], s0_sem.at[b], core)

    def merge(at, n, extra=None):
        total = dp[at : at + n].astype(F32) + r0[at : at + n].astype(F32)
        if extra is not None:
            total = total + extra[...].astype(F32)
        r0[at : at + n] = total.astype(BF16)

    def got_core(b):
        net.got(r0.at[pl.ds(b * 8, 8)], s0_sem.at[b])

    block(2)
    got_core(2)
    merge(16, 8)
    net.push(r0.at[pl.ds(16, 4)], ra, s1_sem.at[0], up)
    net.push(r0.at[pl.ds(20, 4)], rb, s1_sem.at[1], down)
    block(1)
    got_core(1)
    merge(12, 4)
    net.push(r0.at[pl.ds(12, 4)], r2a.at[pl.ds(4, 4)], s1_sem.at[2], up)
    block(3)
    got_core(3)
    merge(24, 4)
    net.push(r0.at[pl.ds(24, 4)], r2b.at[pl.ds(0, 4)], s1_sem.at[3], down)
    block(0)
    net.got(ra, s1_sem.at[0])
    merge(8, 4, ra)
    net.push(r0.at[pl.ds(8, 4)], r2a.at[pl.ds(0, 4)], s1_sem.at[4], up)
    net.got(rb, s1_sem.at[1])
    merge(28, 4, rb)
    net.push(r0.at[pl.ds(28, 4)], r2b.at[pl.ds(4, 4)], s1_sem.at[5], down)
    got_core(0)
    net.got(r2a.at[pl.ds(4, 4)], s1_sem.at[2])
    net.got(r2b.at[pl.ds(0, 4)], s1_sem.at[3])
    net.got(r2a.at[pl.ds(0, 4)], s1_sem.at[4])
    net.got(r2b.at[pl.ds(4, 4)], s1_sem.at[5])

    def own(k):
        return dp[k].astype(F32) + r0[k].astype(F32) + r2a[k].astype(F32) + r2b[k].astype(F32)

    for j in range(1, 8):
        r0[j] = own(j).astype(BF16)
        net.push(r0.at[j], r3.at[8 - j], s2_sem.at[8 - j], here.near(j))
    prompt = own(0)
    for j in range(1, 8):
        net.got(r3.at[j], s2_sem.at[j])
        prompt = prompt + r3[j].astype(F32)
    pg_ref[...] = prompt.astype(BF16)
    grad[0, ROLL:] = prompt.astype(BF16)
    share(prompt_part, prompt_part, gp_sem)

    part = dot(ht[here.c, here.b].reshape(640, 256), grad[0])
    for k in range(1, 8):
        net.got(hx.at[k], h_sem.at[k])
        net.got(roll_part(k), gr_sem.at[k])
        net.got(prompt_part(k), gp_sem.at[k])
        part = part + dot(hx[k].reshape(640, 256), grad[k])
    acc[...] = part.reshape(2, 4, 80, 256)
    wpart[...] = part.astype(BF16).reshape(2, 4, 80, 256)
    for j in range(1, 8):
        s = lax.rem(here.s + j, 8)
        net.push(wpart.at[lax.rem(s, 2), s // 2], wr3.at[8 - j], w_sem.at[8 - j], here.near(j))
    total = acc[here.z, here.a]
    for j in range(1, 8):
        net.got(wr3.at[j], w_sem.at[j])
        total = total + wr3[j].astype(F32)
    wg[0] = total.astype(BF16)
    for j in range(1, 4):
        net.push(wg.at[0], wg.at[4 - j], wg_sem.at[4 - j], here.group(j))
    for j in range(1, 4):
        net.got(wg.at[j], wg_sem.at[j])
        total = total + wg[j].astype(F32)
    w_ref[...] = total
    for copy in stores:
        copy.wait()
    net.drain()


def whole(lengths, q, g, rc, cache, hr, hp):
    vmem, hbm = pl.BlockSpec(memory_space=pltpu.VMEM), pl.BlockSpec(memory_space=pl.ANY)
    dma = pltpu.SemaphoreType.DMA

    def buf(*shape, kind=BF16):
        return pltpu.VMEM(shape, kind)

    scratch = [
        buf(ROWS, HD), buf(ROWS, HD), buf(ROLL, 2 * HD), buf(256, 5120),
        buf(64, 64, 256), buf(HD, KEYS),
        buf(KEYS + ROLL, TILE, kind=F32), buf(KEYS + ROLL, TILE, kind=F32),
        buf(KEYS + ROLL, ROWS), buf(KEYS + ROLL, ROWS),
        buf(ROWS, HD), buf(64, 64, 256),
        buf(2, 4, 2, 4, 80, 256), buf(8, 2, 4, 80, 256), buf(8, 256, 256),
        buf(2, 4, 80, 256, kind=F32), buf(2, 4, 80, 256),
        buf(32, 64, 256), buf(4, 64, 256), buf(4, 64, 256),
        buf(8, 64, 256), buf(8, 64, 256), buf(8, 64, 256),
        buf(8, 80, 256), buf(4, 80, 256),
        dma((28,)), dma((SENDS,)), dma((32,)), dma((32,)), dma((8,)), dma((8,)), dma((8,)),
        dma((4,)), dma((6,)), dma((8,)), dma((8,)), dma((4,)),
    ]
    return pl.pallas_call(
        kernel,
        out_shape=(
            jax.ShapeDtypeStruct((ROLL, HEADS * HD), BF16),
            jax.ShapeDtypeStruct((ROLL, 2 * HD), BF16),
            jax.ShapeDtypeStruct((64, 2 * HD), BF16),
            jax.ShapeDtypeStruct((80, 2 * HD), F32),
        ),
        in_specs=[pl.BlockSpec(memory_space=pltpu.SMEM)] + [hbm] * 6,
        out_specs=(hbm, vmem, vmem, vmem),
        scratch_shapes=scratch,
        compiler_params=pltpu.CompilerParams(
            collective_id=0, has_side_effects=True, vmem_limit_bytes=62 << 20
        ),
    )(lengths, q, g, rc, cache, hr, hp)


def finish_kernel(*refs):
    ins, outs, sems = refs[:4], refs[4:8], refs[8]
    copies = [pltpu.make_async_copy(a, b, sems.at[i]) for i, (a, b) in enumerate(zip(ins, outs))]
    for copy in copies:
        copy.start()
    for copy in copies:
        copy.wait()


def finish(arrays):
    hbm = pl.BlockSpec(memory_space=pl.ANY)
    return pl.pallas_call(
        finish_kernel,
        out_shape=tuple(jax.ShapeDtypeStruct(a.shape, a.dtype) for a in arrays),
        in_specs=[hbm] * 4,
        out_specs=(hbm,) * 4,
        scratch_shapes=[pltpu.SemaphoreType.DMA((4,))],
    )(*arrays)


def body(queries, grad_out, rollout_cache, prompt_cache, rollout_hidden, prompt_hidden, lengths):
    outs = whole(
        lengths, queries[0], grad_out[0], rollout_cache[0], prompt_cache[0], rollout_hidden[0], prompt_hidden[0]
    )
    dq, dr, pg, w = finish(outs)
    return (dq[None], dr[None], pg[None], w)


def solution(mesh):
    rows = P("grp", "ctx", None)
    in_specs = (rows,) * 6 + (P("grp", "ctx"),)
    out_specs = (rows, rows, rows, P("ctx", None))
    return jax.shard_map(body, mesh=mesh, in_specs=in_specs, out_specs=out_specs, check_vma=False)
```

time: 946 us -> 104 us (0.11)
  waiting for transfers between devices: 790 us -> 0 us
  Pallas kernels: 0 us -> 103 us
  matrix products: 88.3 us -> 0 us
  local copies, waits for them, and re-layouts: 36.5 us -> 0 us
  between operations: 14 us -> 0.8 us
    unnamed x5 -> x0, waiting for transfers between devices: 289 us -> none
    reduce_scatter x1 -> x0, waiting for transfers between devices: 283 us -> none  [body(): lax.psum_scatter(buffer, 'ctx', scatter_dimension=0, tiled=True)]
    psum x1 -> x0, waiting for transfers between devices: 112 us -> none  [body(): lax.psum(local_sum.astype(jnp.bfloat16), 'grp').astype(jnp.float32)]
    all_gather x1 -> x0, waiting for transfers between devices: 105 us -> none  [body(): gathered = lax.all_gather(prompt_cache[0], 'ctx', axis=0, tiled=True)]
    pallas_call x0 -> x2, Pallas kernels: none -> 103 us  [the longest x1 83.5 us: whole(): pl.pallas_call(kernel, out_shape=(jax.ShapeDtypeStruct((ROLL, HEADS * HD)...]
    dot_general x63 -> x0, matrix products: 88.3 us -> none  [the longest x16 24.8 us: scores_of(): jnp.einsum('rd,kd->rk', query_rows, keyval[:, :head_size], preferred_elem...]
    dynamic_update_slice x16 -> x0, local copies, waits for them, and re-layouts: 23.4 us -> none  [grad_step(): lax.dynamic_update_slice_in_dim(buffer, terms, index * block_rows, 0)]
  transfers between devices with their start and end apart: 4 -> 0, of which waited for: 4 -> 0; matrix products, arithmetic and copies ran while one was open for 1% -> 0% of each run, Pallas kernels for 0% -> 0%
where the time goes in v2:
time: 104 us
  Pallas kernels  103 us (99%)
    pallas_call x1, Pallas kernels, whole(): pl.pallas_call(kernel, out_shape=(jax.ShapeDtypeStruct((ROLL, HEADS * HD)...  83.5 us
    pallas_call x1, Pallas kernels, finish(): pl.pallas_call(finish_kernel, out_shape=tuple((jax.ShapeDtypeStruct(a.sha...  19.5 us

profile of v2, /device:TPU:8, one launch (start us, length us, event | category | flops | bytes accessed | tf_op | source)
XLA Modules:
  0.0 103.8 jit_solution(5840295887525863793)
XLA Ops:
  0.6 83.5 %shard_map.102 = (bf16[192,1024]{1,0:T(8,128)(2,1)}, bf16[192,256]{1,0:T(8,128)(2,1)}, bf16[64,256]{1,0:T(8,128)(2,1)}, f32[80,256]{1,0:T(8,128)}) custom-call(s32[1,2]{1,0:T(1,128)} %len_ref.1, bf16[192,1024]{1,0:T(8,128)(2,1)} %bitcast.11, bf16[192,1024]{1,0:T(8,128)(2,1)} %bitcast.12, bf16[192,256]{1,0:T(8,128)(2,1)} %bitcast.13, ...), custom_call_target="tpu_custom_call" | custom-call | tf_op jit(solution)/shard_map/pallas_call | solution.py:368
  84.2 19.5 %shard_map.103 = (bf16[192,1024]{1,0:T(8,128)(2,1)}, bf16[192,256]{1,0:T(8,128)(2,1)}, bf16[64,256]{1,0:T(8,128)(2,1)}, f32[80,256]{1,0:T(8,128)}) custom-call(bf16[192,1024]{1,0:T(8,128)(2,1)} %get-tuple-element.12.refs_0_, bf16[192,256]{1,0:T(8,128)(2,1)} %get-tuple-element.13.refs_1_, bf16[64,256]{1,0:T(8,128)(2,1)} %get-tuple-element.14.refs_2_, ...), custom_call_target="tpu_custom_call" | custom-call | tf_op jit(solution)/shard_map/pallas_call | solution.py:396

commit v3 on v2

--- a/solution.py
+++ b/solution.py
@@ -64,11 +64,9 @@
         return ring + near + cross + [self.group(j) for j in range(1, 4)]
 
 
-def barrier(devices):
-    sem = pltpu.get_barrier_semaphore()
+def greet(devices):
     for device in devices:
-        pl.semaphore_signal(sem, inc=1, device_id=device, device_id_type=MESH)
-    pl.semaphore_wait(sem, len(devices))
+        pl.semaphore_signal(pltpu.get_barrier_semaphore(), inc=1, device_id=device, device_id_type=MESH)
 
 
 class Net:
@@ -99,12 +97,13 @@
 def kernel(
     len_ref, q_ref, g_ref, rc_ref, cache_ref, hr_ref, hp_ref,
     dq_ref, dr_ref, pg_ref, w_ref,
-    qa, ga, rc, hbuf, kv, kt, E, DP, PB, DS, dq, dp, ht, hx, grad, acc, wpart,
-    r0, ra, rb, r2a, r2b, r3, wr3, wg,
+    qa, ga, rc, hbuf, kv, kt, E, DP, PB, DS, dq, ht, hx, grad, gp, acc, wpart,
+    r0, ra, rb, r3, wr3, wg,
     local, send, near_sem, core_sem, h_sem, gr_sem, gp_sem, s0_sem, s1_sem, s2_sem, w_sem, wg_sem,
 ):
     here = Place()
     net = Net(send, here)
+    dp, r2a, r2b = hbuf, hbuf.at[:, pl.ds(KEYS, 512)], hbuf.at[:, pl.ds(KEYS + 512, 512)]
     loads = []
 
     def load(src, dst):
@@ -120,30 +119,11 @@
         rows, cols = pl.ds(h * ROLL, ROLL), pl.ds(h * HD, HD)
         load(q_ref.at[:, cols], qa.at[rows])
         load(g_ref.at[:, cols], ga.at[rows])
-    barrier(here.partners())
-
-    loads[0].wait()
-    core = here.cross_a(0)
-    up, down = here.ring(1), here.ring(3)
-    for j in range(1, 8):
-        net.push(kv.at[0], kv.at[8 - j], near_sem.at[8 - j], here.near(j))
-
-    def spread(j):
-        net.push(kv.at[j], kv.at[24 + j], near_sem.at[24 + j], up)
-        net.push(kv.at[j], kv.at[8 + j], near_sem.at[8 + j], down)
-        net.push(kv.at[j], kv.at[32 + j], core_sem.at[j], core)
-
-    def arrived(k):
-        net.got(kv.at[k], near_sem.at[k])
-
-    def to_core(k):
-        net.push(kv.at[k], kv.at[32 + k], core_sem.at[k], core)
-
-    spread(0)
-    for j in range(1, 8):
-        arrived(j)
-        spread(j)
-
+    partners = here.partners()
+    greet(partners)
+
+    grad[:, ROLL:] = jnp.zeros((8, 64, 256), BF16)
+    gp[:, :64] = jnp.zeros((8, 64, 256), BF16)
     loads[1].wait()
     loads[2].wait()
     for k in range(8):
@@ -152,23 +132,47 @@
         for y in range(4):
             ht[0, y, z, x] = part[y, 0]
             ht[1, x, z, y] = part[y, 1]
-        if k < 8:
-            arrived(24 + k)
-            if k < 4:
-                net.push(kv.at[24 + k], kv.at[16 + k], near_sem.at[16 + k], up)
-            to_core(24 + k)
-            arrived(8 + k)
-            if k >= 4:
-                net.push(kv.at[8 + k], kv.at[16 + k], near_sem.at[16 + k], down)
-            to_core(8 + k)
+    pl.semaphore_wait(pltpu.get_barrier_semaphore(), len(partners))
+
+    loads[0].wait()
+    core = here.cross_a(0)
+    up, down = here.ring(1), here.ring(3)
+    for j in range(1, 8):
+        net.push(kv.at[0], kv.at[8 - j], near_sem.at[8 - j], here.near(j))
+
+    def spread(j):
+        net.push(kv.at[j], kv.at[24 + j], near_sem.at[24 + j], up)
+        net.push(kv.at[j], kv.at[8 + j], near_sem.at[8 + j], down)
+        net.push(kv.at[j], kv.at[32 + j], core_sem.at[j], core)
+
+    def arrived(k):
+        net.got(kv.at[k], near_sem.at[k])
+
+    def to_core(k):
+        net.push(kv.at[k], kv.at[32 + k], core_sem.at[k], core)
+
+    spread(0)
+    for j in range(1, 8):
+        arrived(j)
+        spread(j)
+
+    for k in range(8):
+        arrived(24 + k)
+        if k < 4:
+            net.push(kv.at[24 + k], kv.at[16 + k], near_sem.at[16 + k], up)
+        to_core(24 + k)
+        arrived(8 + k)
+        if k >= 4:
+            net.push(kv.at[8 + k], kv.at[16 + k], near_sem.at[16 + k], down)
+        to_core(8 + k)
     for k in range(16, 24):
         arrived(k)
         to_core(k)
     for i in range(1, 4):
-        net.push(ht.at[here.c, lax.rem(here.b + i, 4)], hx.at[4 - i], h_sem.at[4 - i], here.ring(i))
+        net.push(ht.at[here.c, lax.rem(here.b + i, 4)], hx.at[3 - i], h_sem.at[4 - i], here.ring(i))
     for i in range(4):
         slot = 4 + (4 - i) % 4
-        net.push(ht.at[1 - here.c, lax.rem(here.a + i, 4)], hx.at[slot], h_sem.at[slot], here.cross_a(i))
+        net.push(ht.at[1 - here.c, lax.rem(here.a + i, 4)], hx.at[slot - 1], h_sem.at[slot], here.cross_a(i))
     for k in range(32):
         net.got(kv.at[32 + k], core_sem.at[k])
     for copy in loads[3:]:
@@ -223,112 +227,137 @@
         sums = jnp.sum(total * last, axis=0, keepdims=True)
         delta = jnp.broadcast_to(jnp.sum(weighted * last, axis=0, keepdims=True) / sums, (8, TILE))
         inv = live / sums
-        turned = jnp.zeros((HD, TILE), F32)
         for (at, n), old in zip(parts, tops):
             factor = jnp.exp2(old - highest) * inv
             p = E[at : at + n, :].reshape(n // 8, 8, TILE) * factor[None]
             ds = (p * (DP[at : at + n, :].reshape(n // 8, 8, TILE) - delta[None])).reshape(n, TILE).astype(BF16)
             PB[at : at + n, r0_ : r0_ + TILE] = p.reshape(n, TILE).astype(BF16)
             DS[at : at + n, r0_ : r0_ + TILE] = ds
-            turned = turned + dot(kt[:, at : at + n] if at < KEYS else roll_kt, ds)
-        dq[r0_ : r0_ + TILE, :] = (turned.T * SCALE).astype(BF16)
+
+    def query_part(i):
+        cols = slice(i * TILE, (i + 1) * TILE)
+        turned = dot(kt[...], DS[:KEYS, cols]) + dot(roll_kt, DS[KEYS:, cols])
+        dq[cols, :] = (turned.T * SCALE).astype(BF16)
+
+    def grads(at, n):
+        both = [dot(DS[at : at + n, :], qa[...]) * SCALE, dot(PB[at : at + n, :], ga[...])]
+        return jnp.concatenate(both, axis=1).astype(BF16)
+
+    def share(src, dst, sems):
+        for i in range(1, 4):
+            net.push(src(0), dst(4 - i), sems.at[4 - i], here.ring(i))
+        for i in range(4):
+            slot = 4 + (4 - i) % 4
+            net.push(src(0), dst(slot), sems.at[slot], here.cross_a(i))
+
+    def roll_part(k):
+        return grad.at[k, pl.ds(0, ROLL)]
+
+    def prompt_part(k):
+        return gp.at[k, pl.ds(64, 64)]
+
+    mine = grads(KEYS, ROLL)
+    dr_ref[...] = mine
+    grad[0, :ROLL] = mine
+    share(roll_part, roll_part, gr_sem)
+
+    def cell(ref, k):
+        return ref.at[pl.ds(k % 4 * 64, 64), pl.ds(k // 4 * 256, 256)]
+
+    def cells(ref, k, n):
+        return ref.at[:, pl.ds(k // 4 * 256, n // 4 * 256)]
+
+    def block(k):
+        new = grads(k * 512, 512)
+        cells(dp, k * 8, 4)[...] = new[:256]
+        cells(dp, k * 8 + 4, 4)[...] = new[256:]
+
+    def other(b):
+        block(4 + b)
+        net.push(cells(dp, 32 + b * 8, 8), cells(r0, b * 8, 8), s0_sem.at[b], core)
+
+    def merge(at, n, extra=None):
+        total = cells(dp, at, n)[...].astype(F32) + cells(r0, at, n)[...].astype(F32)
+        if extra is not None:
+            total = total + extra[...].astype(F32)
+        cells(r0, at, n)[...] = total.astype(BF16)
+
+    def got_core(b):
+        net.got(cells(r0, b * 8, 8), s0_sem.at[b])
+
+    other(2)
+    block(2)
+    other(1)
+    got_core(2)
+    merge(16, 8)
+    net.push(cells(r0, 16, 4), ra, s1_sem.at[0], up)
+    net.push(cells(r0, 20, 4), rb, s1_sem.at[1], down)
+    other(3)
+    block(1)
+    got_core(1)
+    merge(12, 4)
+    net.push(cells(r0, 12, 4), cells(r2a, 4, 4), s1_sem.at[2], up)
+    block(3)
+    got_core(3)
+    merge(24, 4)
+    net.push(cells(r0, 24, 4), cells(r2b, 0, 4), s1_sem.at[3], down)
+    other(0)
+    net.got(ra, s1_sem.at[0])
+    merge(8, 4, ra)
+    net.push(cells(r0, 8, 4), cells(r2a, 0, 4), s1_sem.at[4], up)
+    net.got(rb, s1_sem.at[1])
+    merge(28, 4, rb)
+    net.push(cells(r0, 28, 4), cells(r2b, 4, 4), s1_sem.at[5], down)
+    block(0)
+    query_part(0)
+    got_core(0)
+    net.got(cells(r2a, 4, 4), s1_sem.at[2])
+    net.got(cells(r2b, 0, 4), s1_sem.at[3])
+    net.got(cells(r2a, 0, 4), s1_sem.at[4])
+    net.got(cells(r2b, 4, 4), s1_sem.at[5])
+
+    def own(k):
+        return sum(cell(ref, k)[...].astype(F32) for ref in (dp, r0, r2a, r2b))
+
+    for j in range(1, 8):
+        cell(r0, j)[...] = own(j).astype(BF16)
+        net.push(cell(r0, j), r3.at[8 - j], s2_sem.at[8 - j], here.near(j))
+    prompt = own(0)
+    query_part(1)
+    query_part(2)
+    for k in range(1, 8):
+        net.got(hx.at[k - 1], h_sem.at[k])
+        net.got(roll_part(k), gr_sem.at[k])
+    part = dot(ht[here.c, here.b].reshape(640, 256), grad[0])
+    for k in range(1, 8):
+        part = part + dot(hx[k - 1].reshape(640, 256), grad[k])
+    acc[...] = part
+    for j in range(1, 8):
+        net.got(r3.at[j], s2_sem.at[j])
+        prompt = prompt + r3[j].astype(F32)
+    pg_ref[...] = prompt.astype(BF16)
+    gp[0, 64:] = prompt.astype(BF16)
+    share(prompt_part, prompt_part, gp_sem)
+
+    query_part(3)
+    query_part(4)
+    part = acc[...] + dot(ht[here.c, here.b, :, :, :, HD:].reshape(640, HD), gp[0])
+    for k in range(1, 8):
+        net.got(prompt_part(k), gp_sem.at[k])
+        part = part + dot(hx[k - 1, :, :, :, HD:].reshape(640, HD), gp[k])
+    acc[...] = part
+    wpart[...] = part.astype(BF16).reshape(2, 4, 80, 256)
+    for j in range(1, 8):
+        s = lax.rem(here.s + j, 8)
+        net.push(wpart.at[lax.rem(s, 2), s // 2], wr3.at[8 - j], w_sem.at[8 - j], here.near(j))
+    query_part(5)
     stores = []
     for h in range(HEADS):
         rows, cols = pl.ds(h * ROLL, ROLL), pl.ds(h * HD, HD)
         copy = pltpu.make_async_copy(dq.at[rows], dq_ref.at[:, cols], local.at[len(loads) + h])
         copy.start()
         stores.append(copy)
-
-    def grads(at, n):
-        both = [dot(DS[at : at + n, :], qa[...]) * SCALE, dot(PB[at : at + n, :], ga[...])]
-        return jnp.concatenate(both, axis=1).astype(BF16)
-
-    def share(src, dst, sems):
-        for i in range(1, 4):
-            net.push(src(0), dst(4 - i), sems.at[4 - i], here.ring(i))
-        for i in range(4):
-            slot = 4 + (4 - i) % 4
-            net.push(src(0), dst(slot), sems.at[slot], here.cross_a(i))
-
-    def roll_part(k):
-        return grad.at[k, pl.ds(0, ROLL)]
-
-    def prompt_part(k):
-        return grad.at[k, pl.ds(ROLL, 64)]
-
-    mine = grads(KEYS, ROLL)
-    dr_ref[...] = mine
-    grad[0, :ROLL] = mine
-    share(roll_part, roll_part, gr_sem)
-
-    def block(k):
-        dp[k * 8 : (k + 1) * 8] = grads(k * 512, 512).reshape(8, 64, 256)
-
-    for i, b in enumerate((2, 1, 3, 0)):
-        block(4 + b)
-        net.push(dp.at[pl.ds(32 + b * 8, 8)], r0.at[pl.ds(b * 8, 8)], s0_sem.at[b], core)
-
-    def merge(at, n, extra=None):
-        total = dp[at : at + n].astype(F32) + r0[at : at + n].astype(F32)
-        if extra is not None:
-            total = total + extra[...].astype(F32)
-        r0[at : at + n] = total.astype(BF16)
-
-    def got_core(b):
-        net.got(r0.at[pl.ds(b * 8, 8)], s0_sem.at[b])
-
-    block(2)
-    got_core(2)
-    merge(16, 8)
-    net.push(r0.at[pl.ds(16, 4)], ra, s1_sem.at[0], up)
-    net.push(r0.at[pl.ds(20, 4)], rb, s1_sem.at[1], down)
-    block(1)
-    got_core(1)
-    merge(12, 4)
-    net.push(r0.at[pl.ds(12, 4)], r2a.at[pl.ds(4, 4)], s1_sem.at[2], up)
-    block(3)
-    got_core(3)
-    merge(24, 4)
-    net.push(r0.at[pl.ds(24, 4)], r2b.at[pl.ds(0, 4)], s1_sem.at[3], down)
-    block(0)
-    net.got(ra, s1_sem.at[0])
-    merge(8, 4, ra)
-    net.push(r0.at[pl.ds(8, 4)], r2a.at[pl.ds(0, 4)], s1_sem.at[4], up)
-    net.got(rb, s1_sem.at[1])
-    merge(28, 4, rb)
-    net.push(r0.at[pl.ds(28, 4)], r2b.at[pl.ds(4, 4)], s1_sem.at[5], down)
-    got_core(0)
-    net.got(r2a.at[pl.ds(4, 4)], s1_sem.at[2])
-    net.got(r2b.at[pl.ds(0, 4)], s1_sem.at[3])
-    net.got(r2a.at[pl.ds(0, 4)], s1_sem.at[4])
-    net.got(r2b.at[pl.ds(4, 4)], s1_sem.at[5])
-
-    def own(k):
-        return dp[k].astype(F32) + r0[k].astype(F32) + r2a[k].astype(F32) + r2b[k].astype(F32)
-
-    for j in range(1, 8):
-        r0[j] = own(j).astype(BF16)
-        net.push(r0.at[j], r3.at[8 - j], s2_sem.at[8 - j], here.near(j))
-    prompt = own(0)
-    for j in range(1, 8):
-        net.got(r3.at[j], s2_sem.at[j])
-        prompt = prompt + r3[j].astype(F32)
-    pg_ref[...] = prompt.astype(BF16)
-    grad[0, ROLL:] = prompt.astype(BF16)
-    share(prompt_part, prompt_part, gp_sem)
-
-    part = dot(ht[here.c, here.b].reshape(640, 256), grad[0])
-    for k in range(1, 8):
-        net.got(hx.at[k], h_sem.at[k])
-        net.got(roll_part(k), gr_sem.at[k])
-        net.got(prompt_part(k), gp_sem.at[k])
-        part = part + dot(hx[k].reshape(640, 256), grad[k])
-    acc[...] = part.reshape(2, 4, 80, 256)
-    wpart[...] = part.astype(BF16).reshape(2, 4, 80, 256)
-    for j in range(1, 8):
-        s = lax.rem(here.s + j, 8)
-        net.push(wpart.at[lax.rem(s, 2), s // 2], wr3.at[8 - j], w_sem.at[8 - j], here.near(j))
-    total = acc[here.z, here.a]
+    total = acc[pl.ds(pl.multiple_of((here.z * 4 + here.a) * 80, 80), 80), :]
     for j in range(1, 8):
         net.got(wr3.at[j], w_sem.at[j])
         total = total + wr3[j].astype(F32)
@@ -356,11 +385,10 @@
         buf(64, 64, 256), buf(HD, KEYS),
         buf(KEYS + ROLL, TILE, kind=F32), buf(KEYS + ROLL, TILE, kind=F32),
         buf(KEYS + ROLL, ROWS), buf(KEYS + ROLL, ROWS),
-        buf(ROWS, HD), buf(64, 64, 256),
-        buf(2, 4, 2, 4, 80, 256), buf(8, 2, 4, 80, 256), buf(8, 256, 256),
-        buf(2, 4, 80, 256, kind=F32), buf(2, 4, 80, 256),
-        buf(32, 64, 256), buf(4, 64, 256), buf(4, 64, 256),
-        buf(8, 64, 256), buf(8, 64, 256), buf(8, 64, 256),
+        buf(ROWS, HD),
+        buf(2, 4, 2, 4, 80, 256), buf(7, 2, 4, 80, 256), buf(8, 256, 256), buf(8, 128, 256),
+        buf(640, 256, kind=F32), buf(2, 4, 80, 256),
+        buf(256, 2048), buf(256, 256), buf(256, 256), buf(8, 64, 256),
         buf(8, 80, 256), buf(4, 80, 256),
         dma((28,)), dma((SENDS,)), dma((32,)), dma((32,)), dma((8,)), dma((8,)), dma((8,)),
         dma((4,)), dma((6,)), dma((8,)), dma((8,)), dma((4,)),
@@ -377,17 +405,21 @@
         out_specs=(hbm, vmem, vmem, vmem),
         scratch_shapes=scratch,
         compiler_params=pltpu.CompilerParams(
-            collective_id=0, has_side_effects=True, vmem_limit_bytes=62 << 20
+            collective_id=0, has_side_effects=True, vmem_limit_bytes=63 << 20
         ),
     )(lengths, q, g, rc, cache, hr, hp)
 
 
 def finish_kernel(*refs):
-    ins, outs, sems = refs[:4], refs[4:8], refs[8]
-    copies = [pltpu.make_async_copy(a, b, sems.at[i]) for i, (a, b) in enumerate(zip(ins, outs))]
-    for copy in copies:
+    ins, outs, bufs, sems = refs[:4], refs[4:8], refs[8:12], refs[12]
+    into = [pltpu.make_async_copy(a, b, sems.at[i]) for i, (a, b) in enumerate(zip(ins, bufs))]
+    out = [pltpu.make_async_copy(b, o, sems.at[4 + i]) for i, (b, o) in enumerate(zip(bufs, outs))]
+    for copy in into:
         copy.start()
-    for copy in copies:
+    for first, second in zip(into, out):
+        first.wait()
+        second.start()
+    for copy in out:
         copy.wait()
 
 
@@ -398,7 +430,7 @@
         out_shape=tuple(jax.ShapeDtypeStruct(a.shape, a.dtype) for a in arrays),
         in_specs=[hbm] * 4,
         out_specs=(hbm,) * 4,
-        scratch_shapes=[pltpu.SemaphoreType.DMA((4,))],
+        scratch_shapes=[pltpu.VMEM(a.shape, a.dtype) for a in arrays] + [pltpu.SemaphoreType.DMA((8,))],
     )(*arrays)
 
 

time: 104 us -> 85.9 us (0.83)
  Pallas kernels: 103 us -> 84.5 us
    pallas_call x1, Pallas kernels: 19.5 us -> 1.87 us  [finish(): pl.pallas_call(finish_kernel, out_shape=tuple((jax.ShapeDtypeStruct(a.sha...]
where the time goes in v3:
time: 85.9 us; the launch traced here: 85.3 us
  Pallas kernels  84.5 us (98%)
    pallas_call x1, Pallas kernels, whole(): pl.pallas_call(kernel, out_shape=(jax.ShapeDtypeStruct((ROLL, HEADS * HD)...  82.6 us
    pallas_call x1, Pallas kernels, finish(): pl.pallas_call(finish_kernel, out_shape=tuple((jax.ShapeDtypeStruct(a.sha...  1.87 us

profile of v3, /device:TPU:8, one launch (start us, length us, event | category | flops | bytes accessed | tf_op | source)
XLA Modules:
  0.0 85.3 jit_solution(14217382501393713048)
XLA Ops:
  0.6 82.6 %shard_map.102 = (bf16[192,1024]{1,0:T(8,128)(2,1)}, bf16[192,256]{1,0:T(8,128)(2,1)}, bf16[64,256]{1,0:T(8,128)(2,1)}, f32[80,256]{1,0:T(8,128)}) custom-call(s32[1,2]{1,0:T(1,128)} %len_ref.1, bf16[192,1024]{1,0:T(8,128)(2,1)} %bitcast.11, bf16[192,1024]{1,0:T(8,128)(2,1)} %bitcast.12, bf16[192,256]{1,0:T(8,128)(2,1)} %bitcast.13, ...), custom_call_target="tpu_custom_call" | custom-call | tf_op jit(solution)/shard_map/pallas_call | solution.py:396
  83.3 1.9 %shard_map.103 = (bf16[192,1024]{1,0:T(8,128)(2,1)}, bf16[192,256]{1,0:T(8,128)(2,1)}, bf16[64,256]{1,0:T(8,128)(2,1)}, f32[80,256]{1,0:T(8,128)}) custom-call(bf16[192,1024]{1,0:T(8,128)(2,1)} %get-tuple-element.12.refs_0_, bf16[192,256]{1,0:T(8,128)(2,1)} %get-tuple-element.13.refs_1_, bf16[64,256]{1,0:T(8,128)(2,1)} %get-tuple-element.14.refs_2_, ...), custom_call_target="tpu_custom_call" | custom-call | tf_op jit(solution)/shard_map/pallas_call | solution.py:428

commit v4 on v3

--- a/solution.py
+++ b/solution.py
@@ -1,3 +1,4 @@
+import functools
 import math
 
 import jax
@@ -91,18 +92,21 @@
             copy.wait_send()
 
 
-SENDS = 63 + 7 + 7 + 7 + 17 + 7 + 3
+SENDS = 63 + 7 + 7 + 14 + 10 + 14 + 14 + 6
+FAR_FIRST = (5, 3, 7, 1, 4, 2, 6)
+SOON_FIRST = (0, 2, 6, 4, 1, 7, 3, 5)
 
 
 def kernel(
     len_ref, q_ref, g_ref, rc_ref, cache_ref, hr_ref, hp_ref,
     dq_ref, dr_ref, pg_ref, w_ref,
-    qa, ga, rc, hbuf, kv, kt, E, DP, PB, DS, dq, ht, hx, grad, gp, acc, wpart,
+    qa, ga, rc, hbuf, kv, kt, E, DP, PB, DS, ht, hx, grad, gp, acc, wpart,
     r0, ra, rb, r3, wr3, wg,
     local, send, near_sem, core_sem, h_sem, gr_sem, gp_sem, s0_sem, s1_sem, s2_sem, w_sem, wg_sem,
 ):
     here = Place()
     net = Net(send, here)
+    dq = qa
     dp, r2a, r2b = hbuf, hbuf.at[:, pl.ds(KEYS, 512)], hbuf.at[:, pl.ds(KEYS + 512, 512)]
     loads = []
 
@@ -137,7 +141,7 @@
     loads[0].wait()
     core = here.cross_a(0)
     up, down = here.ring(1), here.ring(3)
-    for j in range(1, 8):
+    for j in FAR_FIRST:
         net.push(kv.at[0], kv.at[8 - j], near_sem.at[8 - j], here.near(j))
 
     def spread(j):
@@ -152,29 +156,35 @@
         net.push(kv.at[k], kv.at[32 + k], core_sem.at[k], core)
 
     spread(0)
-    for j in range(1, 8):
+    for j in SOON_FIRST[1:]:
         arrived(j)
         spread(j)
 
-    for k in range(8):
-        arrived(24 + k)
-        if k < 4:
-            net.push(kv.at[24 + k], kv.at[16 + k], near_sem.at[16 + k], up)
-        to_core(24 + k)
-        arrived(8 + k)
-        if k >= 4:
-            net.push(kv.at[8 + k], kv.at[16 + k], near_sem.at[16 + k], down)
-        to_core(8 + k)
-    for k in range(16, 24):
-        arrived(k)
-        to_core(k)
-    for i in range(1, 4):
-        net.push(ht.at[here.c, lax.rem(here.b + i, 4)], hx.at[3 - i], h_sem.at[4 - i], here.ring(i))
-    for i in range(4):
-        slot = 4 + (4 - i) % 4
-        net.push(ht.at[1 - here.c, lax.rem(here.a + i, 4)], hx.at[slot - 1], h_sem.at[slot], here.cross_a(i))
-    for k in range(32):
-        net.got(kv.at[32 + k], core_sem.at[k])
+    def pass_on():
+        for i, k in enumerate(SOON_FIRST):
+            arrived(24 + k)
+            if i < 4:
+                net.push(kv.at[24 + k], kv.at[16 + k], near_sem.at[16 + k], up)
+            to_core(24 + k)
+            arrived(8 + k)
+            if i >= 4:
+                net.push(kv.at[8 + k], kv.at[16 + k], near_sem.at[16 + k], down)
+            to_core(8 + k)
+
+    def pass_last():
+        for k in SOON_FIRST:
+            arrived(16 + k)
+            to_core(16 + k)
+        for i in range(1, 4):
+            net.push(ht.at[here.c, lax.rem(here.b + i, 4)], hx.at[3 - i], h_sem.at[4 - i], here.ring(i))
+        for i in range(4):
+            slot = 4 + (4 - i) % 4
+            net.push(ht.at[1 - here.c, lax.rem(here.a + i, 4)], hx.at[slot - 1], h_sem.at[slot], here.cross_a(i))
+
+    def from_core(b):
+        for k in range(8 * b, 8 * b + 8):
+            net.got(kv.at[32 + k], core_sem.at[k])
+
     for copy in loads[3:]:
         copy.wait()
 
@@ -184,11 +194,13 @@
     def values(at, size):
         return kv[at // 64 : (at + size) // 64, :, HD:].reshape(size, HD)
 
-    for c in range(8):
-        kt[:, c * 512 : (c + 1) * 512] = keys(c * 512, 512).T
     roll_kt = rc[:, :HD].T
     n0, n1 = len_ref[0, 0], len_ref[0, 1]
-    parts = [(c * CHUNK, CHUNK) for c in range(KEYS // CHUNK)] + [(KEYS, ROLL)]
+    parts = [(KEYS, ROLL)]
+    for b in (0, 3, 1, 2, 4, 7, 5, 6):
+        parts += [(b * 512, CHUNK), (b * 512 + CHUNK, CHUNK)]
+    due = {3 * 512: pass_on, 2 * 512: pass_last}
+    due.update({(4 + b) * 512: functools.partial(from_core, b) for b in range(4)})
     for r0_ in range(0, ROWS, TILE):
         q, g = qa[r0_ : r0_ + TILE, :], ga[r0_ : r0_ + TILE, :]
         rows = lax.broadcasted_iota(jnp.int32, (1, TILE), 1) + r0_
@@ -206,6 +218,8 @@
         weighted = jnp.zeros((8, TILE), F32)
         tops = []
         for at, n in parts:
+            if r0_ == 0 and at in due:
+                due[at]()
             if at < KEYS:
                 s = dot_nt(keys(at, n), q) * EXP_SCALE
                 d = dot_nt(values(at, n), g)
@@ -234,6 +248,9 @@
             PB[at : at + n, r0_ : r0_ + TILE] = p.reshape(n, TILE).astype(BF16)
             DS[at : at + n, r0_ : r0_ + TILE] = ds
 
+    for c in range(8):
+        kt[:, c * 512 : (c + 1) * 512] = keys(c * 512, 512).T
+
     def query_part(i):
         cols = slice(i * TILE, (i + 1) * TILE)
         turned = dot(kt[...], DS[:KEYS, cols]) + dot(roll_kt, DS[KEYS:, cols])
@@ -243,23 +260,25 @@
         both = [dot(DS[at : at + n, :], qa[...]) * SCALE, dot(PB[at : at + n, :], ga[...])]
         return jnp.concatenate(both, axis=1).astype(BF16)
 
-    def share(src, dst, sems):
-        for i in range(1, 4):
-            net.push(src(0), dst(4 - i), sems.at[4 - i], here.ring(i))
-        for i in range(4):
+    def share(part, sems, first):
+        for i in (2, 1, 3):
+            net.push(part(0), part(4 - i), sems.at[first + 4 - i], here.ring(i))
+        for i in (2, 1, 3, 0):
             slot = 4 + (4 - i) % 4
-            net.push(src(0), dst(slot), sems.at[slot], here.cross_a(i))
+            net.push(part(0), part(slot), sems.at[first + slot], here.cross_a(i))
+
+    def half(h):
+        return pl.ds(h * HD, HD)
 
     def roll_part(k):
         return grad.at[k, pl.ds(0, ROLL)]
 
-    def prompt_part(k):
-        return gp.at[k, pl.ds(64, 64)]
+    def prompt_part(h, k):
+        return gp.at[k, pl.ds(64, 64), half(h)]
 
     mine = grads(KEYS, ROLL)
     dr_ref[...] = mine
     grad[0, :ROLL] = mine
-    share(roll_part, roll_part, gr_sem)
 
     def cell(ref, k):
         return ref.at[pl.ds(k % 4 * 64, 64), pl.ds(k // 4 * 256, 256)]
@@ -321,35 +340,41 @@
 
     for j in range(1, 8):
         cell(r0, j)[...] = own(j).astype(BF16)
-        net.push(cell(r0, j), r3.at[8 - j], s2_sem.at[8 - j], here.near(j))
+    for h in (1, 0):
+        for j in FAR_FIRST:
+            net.push(cell(r0, j).at[:, half(h)], r3.at[7 - j, :, half(h)], s2_sem.at[h * 8 + 8 - j], here.near(j))
+    share(roll_part, gr_sem, 0)
     prompt = own(0)
     query_part(1)
     query_part(2)
+    query_part(3)
+    for h in (1, 0):
+        total = prompt[:, h * HD : (h + 1) * HD]
+        for j in SOON_FIRST[1:]:
+            net.got(r3.at[j - 1, :, half(h)], s2_sem.at[h * 8 + j])
+            total = total + r3[j - 1, :, half(h)].astype(F32)
+        pg_ref[:, half(h)] = total.astype(BF16)
+        prompt_part(h, 0)[...] = total.astype(BF16)
+        share(functools.partial(prompt_part, h), gp_sem, h * 8)
+
+    part = dot(ht[here.c, here.b].reshape(640, 256), grad[0])
     for k in range(1, 8):
         net.got(hx.at[k - 1], h_sem.at[k])
         net.got(roll_part(k), gr_sem.at[k])
-    part = dot(ht[here.c, here.b].reshape(640, 256), grad[0])
-    for k in range(1, 8):
         part = part + dot(hx[k - 1].reshape(640, 256), grad[k])
     acc[...] = part
-    for j in range(1, 8):
-        net.got(r3.at[j], s2_sem.at[j])
-        prompt = prompt + r3[j].astype(F32)
-    pg_ref[...] = prompt.astype(BF16)
-    gp[0, 64:] = prompt.astype(BF16)
-    share(prompt_part, prompt_part, gp_sem)
-
-    query_part(3)
     query_part(4)
-    part = acc[...] + dot(ht[here.c, here.b, :, :, :, HD:].reshape(640, HD), gp[0])
-    for k in range(1, 8):
-        net.got(prompt_part(k), gp_sem.at[k])
-        part = part + dot(hx[k - 1, :, :, :, HD:].reshape(640, HD), gp[k])
-    acc[...] = part
-    wpart[...] = part.astype(BF16).reshape(2, 4, 80, 256)
-    for j in range(1, 8):
-        s = lax.rem(here.s + j, 8)
-        net.push(wpart.at[lax.rem(s, 2), s // 2], wr3.at[8 - j], w_sem.at[8 - j], here.near(j))
+    for h in (1, 0):
+        part = acc[:, half(h)] + dot(ht[here.c, here.b, :, :, :, HD:].reshape(640, HD), gp[0, :, half(h)])
+        for k in range(1, 8):
+            net.got(prompt_part(h, k), gp_sem.at[h * 8 + k])
+            part = part + dot(hx[k - 1, :, :, :, HD:].reshape(640, HD), gp[k, :, half(h)])
+        acc[:, half(h)] = part
+        wpart[:, :, :, half(h)] = part.astype(BF16).reshape(2, 4, 80, HD)
+        for j in FAR_FIRST:
+            s = lax.rem(here.s + j, 8)
+            src = wpart.at[lax.rem(s, 2), s // 2, :, half(h)]
+            net.push(src, wr3.at[7 - j, :, half(h)], w_sem.at[h * 8 + 8 - j], here.near(j))
     query_part(5)
     stores = []
     for h in range(HEADS):
@@ -357,17 +382,22 @@
         copy = pltpu.make_async_copy(dq.at[rows], dq_ref.at[:, cols], local.at[len(loads) + h])
         copy.start()
         stores.append(copy)
-    total = acc[pl.ds(pl.multiple_of((here.z * 4 + here.a) * 80, 80), 80), :]
-    for j in range(1, 8):
-        net.got(wr3.at[j], w_sem.at[j])
-        total = total + wr3[j].astype(F32)
-    wg[0] = total.astype(BF16)
-    for j in range(1, 4):
-        net.push(wg.at[0], wg.at[4 - j], wg_sem.at[4 - j], here.group(j))
-    for j in range(1, 4):
-        net.got(wg.at[j], wg_sem.at[j])
-        total = total + wg[j].astype(F32)
-    w_ref[...] = total
+    totals = {}
+    for h in (1, 0):
+        total = acc[pl.ds(pl.multiple_of((here.z * 4 + here.a) * 80, 80), 80), half(h)]
+        for j in SOON_FIRST[1:]:
+            net.got(wr3.at[j - 1, :, half(h)], w_sem.at[h * 8 + j])
+            total = total + wr3[j - 1, :, half(h)].astype(F32)
+        wg[0, :, half(h)] = total.astype(BF16)
+        for j in (2, 1, 3):
+            net.push(wg.at[0, :, half(h)], wg.at[4 - j, :, half(h)], wg_sem.at[h * 4 + 4 - j], here.group(j))
+        totals[h] = total
+    for h in (1, 0):
+        total = totals[h]
+        for j in (1, 3, 2):
+            net.got(wg.at[j, :, half(h)], wg_sem.at[h * 4 + j])
+            total = total + wg[j, :, half(h)].astype(F32)
+        w_ref[:, half(h)] = total
     for copy in stores:
         copy.wait()
     net.drain()
@@ -385,13 +415,12 @@
         buf(64, 64, 256), buf(HD, KEYS),
         buf(KEYS + ROLL, TILE, kind=F32), buf(KEYS + ROLL, TILE, kind=F32),
         buf(KEYS + ROLL, ROWS), buf(KEYS + ROLL, ROWS),
-        buf(ROWS, HD),
         buf(2, 4, 2, 4, 80, 256), buf(7, 2, 4, 80, 256), buf(8, 256, 256), buf(8, 128, 256),
         buf(640, 256, kind=F32), buf(2, 4, 80, 256),
-        buf(256, 2048), buf(256, 256), buf(256, 256), buf(8, 64, 256),
-        buf(8, 80, 256), buf(4, 80, 256),
-        dma((28,)), dma((SENDS,)), dma((32,)), dma((32,)), dma((8,)), dma((8,)), dma((8,)),
-        dma((4,)), dma((6,)), dma((8,)), dma((8,)), dma((4,)),
+        buf(256, 2048), buf(256, 256), buf(256, 256), buf(7, 64, 256),
+        buf(7, 80, 256), buf(4, 80, 256),
+        dma((28,)), dma((SENDS,)), dma((32,)), dma((32,)), dma((8,)), dma((8,)), dma((16,)),
+        dma((4,)), dma((6,)), dma((16,)), dma((16,)), dma((8,)),
     ]
     return pl.pallas_call(
         kernel,
@@ -405,7 +434,7 @@
         out_specs=(hbm, vmem, vmem, vmem),
         scratch_shapes=scratch,
         compiler_params=pltpu.CompilerParams(
-            collective_id=0, has_side_effects=True, vmem_limit_bytes=63 << 20
+            collective_id=0, has_side_effects=True, vmem_limit_bytes=(63 << 20) + (512 << 10)
         ),
     )(lengths, q, g, rc, cache, hr, hp)
 

time: 85.9 us -> 83.9 us (0.977)
  Pallas kernels: 84.5 us -> 82.9 us
    pallas_call x1, Pallas kernels: 82.6 us -> 81.1 us  [whole(): pl.pallas_call(kernel, out_shape=(jax.ShapeDtypeStruct((ROLL, HEADS * HD)...]
where the time goes in v4:
time: 83.9 us; the launch traced here: 83.8 us
  Pallas kernels  82.9 us (99%)
    pallas_call x1, Pallas kernels, whole(): pl.pallas_call(kernel, out_shape=(jax.ShapeDtypeStruct((ROLL, HEADS * HD)...  81.1 us
    pallas_call x1, Pallas kernels, finish(): pl.pallas_call(finish_kernel, out_shape=tuple((jax.ShapeDtypeStruct(a.sha...  1.87 us

profile of v4, /device:TPU:8, one launch (start us, length us, event | category | flops | bytes accessed | tf_op | source)
XLA Modules:
  0.0 83.8 jit_solution(1595517089216650321)
XLA Ops:
  0.6 81.1 %shard_map.102 = (bf16[192,1024]{1,0:T(8,128)(2,1)}, bf16[192,256]{1,0:T(8,128)(2,1)}, bf16[64,256]{1,0:T(8,128)(2,1)}, f32[80,256]{1,0:T(8,128)}) custom-call(s32[1,2]{1,0:T(1,128)} %len_ref.1, bf16[192,1024]{1,0:T(8,128)(2,1)} %bitcast.11, bf16[192,1024]{1,0:T(8,128)(2,1)} %bitcast.12, bf16[192,256]{1,0:T(8,128)(2,1)} %bitcast.13, ...), custom_call_target="tpu_custom_call" | custom-call | tf_op jit(solution)/shard_map/pallas_call | solution.py:425
  81.7 1.9 %shard_map.103 = (bf16[192,1024]{1,0:T(8,128)(2,1)}, bf16[192,256]{1,0:T(8,128)(2,1)}, bf16[64,256]{1,0:T(8,128)(2,1)}, f32[80,256]{1,0:T(8,128)}) custom-call(bf16[192,1024]{1,0:T(8,128)(2,1)} %get-tuple-element.12.refs_0_, bf16[192,256]{1,0:T(8,128)(2,1)} %get-tuple-element.13.refs_1_, bf16[64,256]{1,0:T(8,128)(2,1)} %get-tuple-element.14.refs_2_, ...), custom_call_target="tpu_custom_call" | custom-call | tf_op jit(solution)/shard_map/pallas_call | solution.py:457

commit v5 on v4

--- a/solution.py
+++ b/solution.py
@@ -363,7 +363,6 @@
         net.got(roll_part(k), gr_sem.at[k])
         part = part + dot(hx[k - 1].reshape(640, 256), grad[k])
     acc[...] = part
-    query_part(4)
     for h in (1, 0):
         part = acc[:, half(h)] + dot(ht[here.c, here.b, :, :, :, HD:].reshape(640, HD), gp[0, :, half(h)])
         for k in range(1, 8):
@@ -375,6 +374,7 @@
             s = lax.rem(here.s + j, 8)
             src = wpart.at[lax.rem(s, 2), s // 2, :, half(h)]
             net.push(src, wr3.at[7 - j, :, half(h)], w_sem.at[h * 8 + 8 - j], here.near(j))
+    query_part(4)
     query_part(5)
     stores = []
     for h in range(HEADS):

time: 83.9 us -> 84.5 us (level)
  no operation moved by 1% of the time
where the time goes in v5:
time: 84.5 us; the launch traced here: 84.4 us
  Pallas kernels  83.6 us (99%)
    pallas_call x1, Pallas kernels, whole(): pl.pallas_call(kernel, out_shape=(jax.ShapeDtypeStruct((ROLL, HEADS * HD)...  81.7 us
    pallas_call x1, Pallas kernels, finish(): pl.pallas_call(finish_kernel, out_shape=tuple((jax.ShapeDtypeStruct(a.sha...  1.87 us

profile of v5, /device:TPU:8, one launch (start us, length us, event | category | flops | bytes accessed | tf_op | source)
XLA Modules:
  0.0 84.4 jit_solution(6017771826312279761)
XLA Ops:
  0.6 81.7 %shard_map.102 = (bf16[192,1024]{1,0:T(8,128)(2,1)}, bf16[192,256]{1,0:T(8,128)(2,1)}, bf16[64,256]{1,0:T(8,128)(2,1)}, f32[80,256]{1,0:T(8,128)}) custom-call(s32[1,2]{1,0:T(1,128)} %len_ref.1, bf16[192,1024]{1,0:T(8,128)(2,1)} %bitcast.11, bf16[192,1024]{1,0:T(8,128)(2,1)} %bitcast.12, bf16[192,256]{1,0:T(8,128)(2,1)} %bitcast.13, ...), custom_call_target="tpu_custom_call" | custom-call | tf_op jit(solution)/shard_map/pallas_call | solution.py:425
  82.4 1.9 %shard_map.103 = (bf16[192,1024]{1,0:T(8,128)(2,1)}, bf16[192,256]{1,0:T(8,128)(2,1)}, bf16[64,256]{1,0:T(8,128)(2,1)}, f32[80,256]{1,0:T(8,128)}) custom-call(bf16[192,1024]{1,0:T(8,128)(2,1)} %get-tuple-element.12.refs_0_, bf16[192,256]{1,0:T(8,128)(2,1)} %get-tuple-element.13.refs_1_, bf16[64,256]{1,0:T(8,128)(2,1)} %get-tuple-element.14.refs_2_, ...), custom_call_target="tpu_custom_call" | custom-call | tf_op jit(solution)/shard_map/pallas_call | solution.py:457
